TPU v7x, 32 devices: a whole 2x2x4 slice. The times are simulated.
32 devices in a mesh: dp: 2 (over x), expert: 16 (over z, y, core).
Axes of the slice: x: 2, y: 2, z: 4, core: 2. Of those that a mesh axis runs over, the one named last changes fastest.
Arguments:
- tokens: bfloat16 [32, 576, 768], P(('dp', 'expert')), may hold values from -6 to 6
- cotangent: bfloat16 [32, 576, 768], P(('dp', 'expert')), may hold values from -6 to 6
- expert_choice: int32 [32, 576, 2], P(('dp', 'expert')), may hold values from 0 to 15, all different within a row
- priority: int32 [32, 576], P(('dp', 'expert')), may hold values from 0 to 575, each once within a row
- projection: float32 [768, 2304], P(('dp', 'expert')), may hold values from -1 to 1
- projection_first: float32 [768, 2304], P(('dp', 'expert'))
- projection_second: float32 [768, 2304], P(('dp', 'expert'))
- output_weight: float32 [768, 768], P(('dp', 'expert')), may hold values from -2.5 to 2.5
- output_first: float32 [768, 768], P(('dp', 'expert'))
- output_second: float32 [768, 768], P(('dp', 'expert'))
- router_weight: float32 [768, 16], P(('dp', 'expert')), may hold values from -0.125 to 0.125
- router_first: float32 [768, 16], P(('dp', 'expert'))
- router_second: float32 [768, 16], P(('dp', 'expert'))
- vectors: float32 [7, 768], P(None, ('dp', 'expert')), may hold values from -0.4 to 2.5
- vectors_first: float32 [7, 768], P(None, ('dp', 'expert'))
- vectors_second: float32 [7, 768], P(None, ('dp', 'expert'))
- expert_inner: float32 [16, 768, 3072], P('expert', None, 'dp'), may hold values from -0.21875 to 0.21875
- inner_first: float32 [16, 768, 3072], P('expert', None, 'dp')
- inner_second: float32 [16, 768, 3072], P('expert', None, 'dp')
- hidden_bias: float32 [16, 3072], P('expert', 'dp'), may hold values from -0.6 to 0.6
- hidden_first: float32 [16, 3072], P('expert', 'dp')
- hidden_second: float32 [16, 3072], P('expert', 'dp')
- expert_outer: float32 [16, 3072, 768], P('expert', 'dp'), may hold values from -1.75 to 1.75
- outer_first: float32 [16, 3072, 768], P('expert', 'dp')
- outer_second: float32 [16, 3072, 768], P('expert', 'dp')
- return_bias: float32 [16, 768], P('expert', 'dp'), may hold values from -6 to 6
- return_first: float32 [16, 768], P('expert', 'dp')
- return_second: float32 [16, 768], P('expert', 'dp')
Outputs:
- block_output: bfloat16 [32, 576, 768], P(('dp', 'expert'))
- input_grad: float32 [32, 576, 768], P(('dp', 'expert'))
- grad_norm: float32 [], replicated
- projection_next: float32 [768, 2304], P(('dp', 'expert'))
- projection_moment: float32 [768, 2304], P(('dp', 'expert'))
- projection_square: float32 [768, 2304], P(('dp', 'expert'))
- output_next: float32 [768, 768], P(('dp', 'expert'))
- output_moment: float32 [768, 768], P(('dp', 'expert'))
- output_square: float32 [768, 768], P(('dp', 'expert'))
- router_next: float32 [768, 16], P(('dp', 'expert'))
- router_moment: float32 [768, 16], P(('dp', 'expert'))
- router_square: float32 [768, 16], P(('dp', 'expert'))
- vectors_next: float32 [7, 768], P(None, ('dp', 'expert'))
- vectors_moment: float32 [7, 768], P(None, ('dp', 'expert'))
- vectors_square: float32 [7, 768], P(None, ('dp', 'expert'))
- inner_next: float32 [16, 768, 3072], P('expert', None, 'dp')
- inner_moment: float32 [16, 768, 3072], P('expert', None, 'dp')
- inner_square: float32 [16, 768, 3072], P('expert', None, 'dp')
- hidden_next: float32 [16, 3072], P('expert', 'dp')
- hidden_moment: float32 [16, 3072], P('expert', 'dp')
- hidden_square: float32 [16, 3072], P('expert', 'dp')
- outer_next: float32 [16, 3072, 768], P('expert', 'dp')
- outer_moment: float32 [16, 3072, 768], P('expert', 'dp')
- outer_square: float32 [16, 3072, 768], P('expert', 'dp')
- return_next: float32 [16, 768], P('expert', 'dp')
- return_moment: float32 [16, 768], P('expert', 'dp')
- return_square: float32 [16, 768], P('expert', 'dp')
Inputs may be any that keep to these rules, and one draw needn't show every extreme that they name: `expert_choice`: the 2 experts of a patch are all different. `priority`: in each image every number from 0 to 575 stands once; a lower number claims expert slots earlier.
All inputs are finite; a program needn't handle non-finite values.
Results may differ from a plain program's by a relative error of at most 0.025.
Values may be sent and summed in bfloat16 or wider, within the bound.
A program may use at most 256 MiB of HBM per device.

v0:
```python
import jax
import jax.numpy as jnp
from jax import lax
from jax.sharding import PartitionSpec as P

HEADS = 12
HEAD_DIM = 64
STEP = 10


NORM_EPS = 1e-06
ADAM_EPS = 1e-08
BETA_ONE = 0.9
BETA_TWO = 0.999
DECAY = 0.1
THRESHOLD = 1.0
RATE_PROJECTION = 0.1
RATE_OUTPUT = 1.0
RATE_ROUTER = 0.05
RATE_VECTORS = 0.5
RATE_INNER = 0.1
RATE_HIDDEN = 0.25
RATE_OUTER = 1.5
RATE_RETURN = 2.0


def layer_norm(values, norm_gain, norm_bias):
    center = values - jnp.mean(values, axis=-1, keepdims=True)
    spread = jnp.mean(center * center, axis=-1, keepdims=True)
    return center * lax.rsqrt(spread + NORM_EPS) * norm_gain + norm_bias


def smooth_gate(values):
    return jax.nn.gelu(values, approximate=True)


def mixed_dot(left, right):
    return jnp.dot(left, right, preferred_element_type=jnp.float32)


def rows_product(left, right):
    return lax.dot_general(
        left, right, (((0,), (0,)), ((), ())), preferred_element_type=jnp.float32
    )


def columns_product(left, right):
    return lax.dot_general(
        left, right, (((1,), (1,)), ((), ())), preferred_element_type=jnp.float32
    )


def assign_slots(chosen, claim_order, expert_count, capacity):
    patches = chosen.shape[0]
    top_count = chosen.shape[1]
    claim_rank = (
        jnp.arange(top_count, dtype=jnp.int32)[None, :] * patches + claim_order[:, None]
    ).T.reshape(-1)
    flat_choice = chosen.T.reshape(-1)
    onehot = (flat_choice[:, None] == jnp.arange(expert_count, dtype=jnp.int32)[None, :]).astype(
        jnp.float32
    )
    earlier = (claim_rank[None, :] < claim_rank[:, None]).astype(jnp.float32)
    counts = jnp.dot(
        earlier, onehot, precision=lax.Precision.HIGHEST, preferred_element_type=jnp.float32
    )
    position = jnp.sum(counts * onehot, axis=1).astype(jnp.int32).reshape(top_count, patches).T
    kept_mask = position < capacity
    flat_slot = chosen * capacity + jnp.minimum(position, capacity - 1)
    return (flat_slot, kept_mask)


def slot_matches(flat_slot, kept_mask, slot_count):
    slot_ids = jnp.arange(slot_count, dtype=jnp.int32)
    return (flat_slot[None, :, :] == slot_ids[:, None, None]) & kept_mask[None, :, :]


def select_gates(logits, chosen, expert_count):
    router_probs = jax.nn.softmax(logits, axis=-1)
    onehot = chosen[:, :, None] == jnp.arange(expert_count, dtype=jnp.int32)[None, None, :]
    return jnp.sum(jnp.where(onehot, router_probs[:, None, :], 0.0), axis=2)


def adam_update(weight, first_state, second, gradient, clip_factor, step_rate, decay_rate):
    scaled = gradient * clip_factor
    first_new = BETA_ONE * first_state + (1.0 - BETA_ONE) * scaled
    second_new = BETA_TWO * second + (1.0 - BETA_TWO) * scaled * scaled
    first_hat = first_new / (1.0 - BETA_ONE**STEP)
    second_hat = second_new / (1.0 - BETA_TWO**STEP)
    weight_new = weight - step_rate * (
        first_hat / (jnp.sqrt(second_hat) + ADAM_EPS) + decay_rate * weight
    )
    return (weight_new, first_new, second_new)


def shards(
    tokens,
    cotangent,
    expert_choice,
    priority,
    projection,
    projection_first,
    projection_second,
    output_weight,
    output_first,
    output_second,
    router_weight,
    router_first,
    router_second,
    vectors,
    vectors_first,
    vectors_second,
    expert_inner,
    inner_first,
    inner_second,
    hidden_bias,
    hidden_first,
    hidden_second,
    expert_outer,
    outer_first,
    outer_second,
    return_bias,
    return_first,
    return_second,
):
    model_width = tokens.shape[2]
    patches = tokens.shape[1]
    experts = lax.axis_size("expert")
    capacity = max(2, patches // experts)
    slot_count = experts * capacity
    score_scale = HEAD_DIM ** (-0.5)
    dense_shards = (
        projection.astype(jnp.bfloat16),
        output_weight.astype(jnp.bfloat16),
        router_weight.astype(jnp.bfloat16),
        vectors.astype(jnp.bfloat16),
    )
    partial_shards = (
        lax.all_gather(dense_shards[0], "expert", axis=0, tiled=True),
        lax.all_gather(dense_shards[1], "expert", axis=0, tiled=True),
        lax.all_gather(dense_shards[2], "expert", axis=0, tiled=True),
        lax.all_gather(dense_shards[3], "expert", axis=1, tiled=True),
    )
    whole_projection, whole_output, whole_router, whole_vectors = (
        lax.all_gather(partial_shards[0], "dp", axis=0, tiled=True),
        lax.all_gather(partial_shards[1], "dp", axis=0, tiled=True),
        lax.all_gather(partial_shards[2], "dp", axis=0, tiled=True),
        lax.all_gather(partial_shards[3], "dp", axis=1, tiled=True),
    )
    inner_low = expert_inner.astype(jnp.bfloat16)
    hidden_low = hidden_bias.astype(jnp.bfloat16)
    outer_low = expert_outer.astype(jnp.bfloat16)
    return_low = return_bias.astype(jnp.bfloat16)
    inner_all, hidden_all, outer_all, return_all = (
        lax.all_gather(inner_low, "dp", axis=2, tiled=True),
        lax.all_gather(hidden_low, "dp", axis=1, tiled=True),
        lax.all_gather(outer_low, "dp", axis=1, tiled=True),
        lax.all_gather(return_low, "dp", axis=1, tiled=True),
    )
    vector_rows = whole_vectors.astype(jnp.float32)
    image_rows = tokens[0].astype(jnp.float32)
    normed_one, norm_back_one = jax.vjp(layer_norm, image_rows, vector_rows[0], vector_rows[1])
    normed_low = normed_one.astype(jnp.bfloat16)
    projected = mixed_dot(normed_low, whole_projection)
    queries = (
        (projected[:, :model_width] + vector_rows[2])
        .astype(jnp.bfloat16)
        .reshape(patches, HEADS, HEAD_DIM)
    )
    key_rows = (
        projected[:, model_width : 2 * model_width]
        .astype(jnp.bfloat16)
        .reshape(patches, HEADS, HEAD_DIM)
    )
    value_rows = (
        (projected[:, 2 * model_width :] + vector_rows[3])
        .astype(jnp.bfloat16)
        .reshape(patches, HEADS, HEAD_DIM)
    )
    scores = (
        jnp.einsum("qhd,khd->hqk", queries, key_rows, preferred_element_type=jnp.float32)
        * score_scale
    )
    score_top = jnp.max(scores, axis=-1, keepdims=True)
    raised = jnp.exp(scores - score_top)
    totals = jnp.sum(raised, axis=-1, keepdims=True)
    attention = raised / totals
    log_total = score_top + jnp.log(totals)
    context = (
        jnp.einsum(
            "hqk,khd->qhd",
            attention.astype(jnp.bfloat16),
            value_rows,
            preferred_element_type=jnp.float32,
        )
        .reshape(patches, model_width)
        .astype(jnp.bfloat16)
    )
    middle = image_rows + (mixed_dot(context, whole_output) + vector_rows[4])
    normed_two, norm_back_two = jax.vjp(layer_norm, middle, vector_rows[5], vector_rows[6])
    second_low = normed_two.astype(jnp.bfloat16)
    logits = mixed_dot(second_low, whole_router)
    chosen = expert_choice[0]

    def gate_choice(values):
        return select_gates(values, chosen, experts)

    gate_values, gate_back = jax.vjp(gate_choice, logits)
    flat_slot, kept_mask = assign_slots(chosen, priority[0], experts, capacity)
    matches = slot_matches(flat_slot, kept_mask, slot_count)
    slot_table = jnp.any(matches, axis=2).astype(jnp.bfloat16)
    dispatched = (
        mixed_dot(slot_table, second_low)
        .astype(jnp.bfloat16)
        .reshape(experts, capacity, model_width)
    )
    arrived = lax.all_to_all(dispatched, "expert", split_axis=0, concat_axis=0, tiled=True).reshape(
        slot_count, model_width
    )
    pre_act = mixed_dot(arrived, inner_all[0]) + hidden_all[0].astype(jnp.float32)
    activated, gelu_back = jax.vjp(smooth_gate, pre_act)
    active_low = activated.astype(jnp.bfloat16)
    expert_out = (mixed_dot(active_low, outer_all[0]) + return_all[0].astype(jnp.float32)).astype(
        jnp.bfloat16
    )
    returned = lax.all_to_all(
        expert_out.reshape(experts, capacity, model_width),
        "expert",
        split_axis=0,
        concat_axis=0,
        tiled=True,
    ).reshape(slot_count, model_width)
    picked = returned[flat_slot].astype(jnp.float32)
    weighted = jnp.where(kept_mask, gate_values, 0.0)
    final = middle + jnp.sum(weighted[:, :, None] * picked, axis=1)
    block_output = final.astype(jnp.bfloat16)[None]
    upstream = cotangent[0].astype(jnp.float32)
    gate_grad = jnp.where(kept_mask, jnp.sum(upstream[:, None, :] * picked, axis=2), 0.0)
    slot_gate = jnp.sum(jnp.where(matches, weighted[None, :, :], 0.0), axis=(1, 2))
    slot_grad = (mixed_dot(slot_table, cotangent[0]) * slot_gate[:, None]).astype(jnp.bfloat16)
    sent_grad = lax.all_to_all(
        slot_grad.reshape(experts, capacity, model_width),
        "expert",
        split_axis=0,
        concat_axis=0,
        tiled=True,
    ).reshape(slot_count, model_width)
    outer_grad = rows_product(active_low, sent_grad)
    return_grad = jnp.sum(sent_grad, axis=0, dtype=jnp.float32)
    active_grad = columns_product(sent_grad, outer_all[0])
    (pre_grad,) = gelu_back(active_grad)
    pre_low = pre_grad.astype(jnp.bfloat16)
    inner_grad = rows_product(arrived, pre_low)
    hidden_grad = jnp.sum(pre_low, axis=0, dtype=jnp.float32)
    row_grad = columns_product(pre_low, inner_all[0]).astype(jnp.bfloat16)
    expert_grads = (
        lax.psum_scatter(
            inner_grad[None].astype(jnp.bfloat16), "dp", scatter_dimension=2, tiled=True
        ).astype(jnp.float32),
        lax.psum_scatter(
            hidden_grad[None].astype(jnp.bfloat16), "dp", scatter_dimension=1, tiled=True
        ).astype(jnp.float32),
        lax.psum_scatter(
            outer_grad[None].astype(jnp.bfloat16), "dp", scatter_dimension=1, tiled=True
        ).astype(jnp.float32),
        lax.psum_scatter(
            return_grad[None].astype(jnp.bfloat16), "dp", scatter_dimension=1, tiled=True
        ).astype(jnp.float32),
    )
    back_rows = lax.all_to_all(
        row_grad.reshape(experts, capacity, model_width),
        "expert",
        split_axis=0,
        concat_axis=0,
        tiled=True,
    ).reshape(slot_count, model_width)
    (logit_grad,) = gate_back(gate_grad)
    logit_low = logit_grad.astype(jnp.bfloat16)
    router_grad = rows_product(second_low, logit_low)
    second_grad = rows_product(slot_table, back_rows) + columns_product(logit_low, whole_router)
    middle_part, gain_two_grad, bias_two_grad = norm_back_two(second_grad)
    middle_grad = upstream + middle_part
    branch_low = middle_grad.astype(jnp.bfloat16)
    output_grad = rows_product(context, branch_low)
    out_bias_grad = jnp.sum(branch_low, axis=0, dtype=jnp.float32)
    context_grad = (
        columns_product(branch_low, whole_output)
        .astype(jnp.bfloat16)
        .reshape(patches, HEADS, HEAD_DIM)
    )
    scores = (
        jnp.einsum("qhd,khd->hqk", queries, key_rows, preferred_element_type=jnp.float32)
        * score_scale
    )
    attention = jnp.exp(scores - log_total)
    attention_grad = jnp.einsum(
        "qhd,khd->hqk", context_grad, value_rows, preferred_element_type=jnp.float32
    )
    value_grad = jnp.einsum(
        "hqk,qhd->khd",
        attention.astype(jnp.bfloat16),
        context_grad,
        preferred_element_type=jnp.float32,
    ).astype(jnp.bfloat16)
    centered = jnp.sum(attention * attention_grad, axis=-1, keepdims=True)
    score_grad = (attention * (attention_grad - centered)).astype(jnp.bfloat16)
    query_grad = (
        (
            jnp.einsum("hqk,khd->qhd", score_grad, key_rows, preferred_element_type=jnp.float32)
            * score_scale
        )
        .astype(jnp.bfloat16)
        .reshape(patches, model_width)
    )
    key_grad = (
        (
            jnp.einsum("hqk,qhd->khd", score_grad, queries, preferred_element_type=jnp.float32)
            * score_scale
        )
        .astype(jnp.bfloat16)
        .reshape(patches, model_width)
    )
    value_flat = value_grad.reshape(patches, model_width)
    joined_grad = jnp.concatenate([query_grad, key_grad, value_flat], axis=1)
    projection_grad = rows_product(normed_low, joined_grad)
    normed_grad = columns_product(joined_grad, whole_projection)
    input_part, gain_one_grad, bias_one_grad = norm_back_one(normed_grad)
    input_grad = (middle_grad + input_part)[None]
    vector_grad = jnp.stack(
        [
            gain_one_grad,
            bias_one_grad,
            jnp.sum(query_grad, axis=0, dtype=jnp.float32),
            jnp.sum(value_flat, axis=0, dtype=jnp.float32),
            out_bias_grad,
            gain_two_grad,
            bias_two_grad,
        ]
    )
    local_grads = (projection_grad, output_grad, router_grad, vector_grad)
    partial_grads = (
        lax.psum_scatter(
            local_grads[0].astype(jnp.bfloat16), "dp", scatter_dimension=0, tiled=True
        ).astype(jnp.float32),
        lax.psum_scatter(
            local_grads[1].astype(jnp.bfloat16), "dp", scatter_dimension=0, tiled=True
        ).astype(jnp.float32),
        lax.psum_scatter(
            local_grads[2].astype(jnp.bfloat16), "dp", scatter_dimension=0, tiled=True
        ).astype(jnp.float32),
        lax.psum_scatter(
            local_grads[3].astype(jnp.bfloat16), "dp", scatter_dimension=1, tiled=True
        ).astype(jnp.float32),
    )
    dense_grads = (
        lax.psum_scatter(
            partial_grads[0].astype(jnp.bfloat16), "expert", scatter_dimension=0, tiled=True
        ).astype(jnp.float32),
        lax.psum_scatter(
            partial_grads[1].astype(jnp.bfloat16), "expert", scatter_dimension=0, tiled=True
        ).astype(jnp.float32),
        lax.psum_scatter(
            partial_grads[2].astype(jnp.bfloat16), "expert", scatter_dimension=0, tiled=True
        ).astype(jnp.float32),
        lax.psum_scatter(
            partial_grads[3].astype(jnp.bfloat16), "expert", scatter_dimension=1, tiled=True
        ).astype(jnp.float32),
    )
    all_grads = tuple(dense_grads) + tuple(expert_grads)
    local_square = jnp.sum(all_grads[0] * all_grads[0])
    for gradient in all_grads[1:]:
        local_square = local_square + jnp.sum(gradient * gradient)
    square_total = lax.psum(local_square, ("dp", "expert"))
    grad_norm = jnp.sqrt(square_total)
    clip_factor = THRESHOLD / jnp.maximum(grad_norm, THRESHOLD)
    projection_next, projection_moment, projection_square = adam_update(
        projection,
        projection_first,
        projection_second,
        all_grads[0],
        clip_factor,
        RATE_PROJECTION,
        DECAY,
    )
    output_next, output_moment, output_square = adam_update(
        output_weight, output_first, output_second, all_grads[1], clip_factor, RATE_OUTPUT, DECAY
    )
    router_next, router_moment, router_square = adam_update(
        router_weight, router_first, router_second, all_grads[2], clip_factor, RATE_ROUTER, DECAY
    )
    vectors_next, vectors_moment, vectors_square = adam_update(
        vectors, vectors_first, vectors_second, all_grads[3], clip_factor, RATE_VECTORS, 0.0
    )
    inner_next, inner_moment, inner_square = adam_update(
        expert_inner, inner_first, inner_second, all_grads[4], clip_factor, RATE_INNER, DECAY
    )
    hidden_next, hidden_moment, hidden_square = adam_update(
        hidden_bias, hidden_first, hidden_second, all_grads[5], clip_factor, RATE_HIDDEN, 0.0
    )
    outer_next, outer_moment, outer_square = adam_update(
        expert_outer, outer_first, outer_second, all_grads[6], clip_factor, RATE_OUTER, DECAY
    )
    return_next, return_moment, return_square = adam_update(
        return_bias, return_first, return_second, all_grads[7], clip_factor, RATE_RETURN, 0.0
    )
    return (
        block_output,
        input_grad,
        grad_norm,
        projection_next,
        projection_moment,
        projection_square,
        output_next,
        output_moment,
        output_square,
        router_next,
        router_moment,
        router_square,
        vectors_next,
        vectors_moment,
        vectors_square,
        inner_next,
        inner_moment,
        inner_square,
        hidden_next,
        hidden_moment,
        hidden_square,
        outer_next,
        outer_moment,
        outer_square,
        return_next,
        return_moment,
        return_square,
    )


def solution(mesh):
    return jax.shard_map(
        shards,
        mesh=mesh,
        in_specs=(
            P(("dp", "expert"), None, None),
            P(("dp", "expert"), None, None),
            P(("dp", "expert"), None, None),
            P(("dp", "expert"), None),
            P(("dp", "expert"), None),
            P(("dp", "expert"), None),
            P(("dp", "expert"), None),
            P(("dp", "expert"), None),
            P(("dp", "expert"), None),
            P(("dp", "expert"), None),
            P(("dp", "expert"), None),
            P(("dp", "expert"), None),
            P(("dp", "expert"), None),
            P(None, ("dp", "expert")),
            P(None, ("dp", "expert")),
            P(None, ("dp", "expert")),
            P("expert", None, "dp"),
            P("expert", None, "dp"),
            P("expert", None, "dp"),
            P("expert", "dp"),
            P("expert", "dp"),
            P("expert", "dp"),
            P("expert", "dp", None),
            P("expert", "dp", None),
            P("expert", "dp", None),
            P("expert", "dp"),
            P("expert", "dp"),
            P("expert", "dp"),
        ),
        out_specs=(
            P(("dp", "expert"), None, None),
            P(("dp", "expert"), None, None),
            P(),
            P(("dp", "expert"), None),
            P(("dp", "expert"), None),
            P(("dp", "expert"), None),
            P(("dp", "expert"), None),
            P(("dp", "expert"), None),
            P(("dp", "expert"), None),
            P(("dp", "expert"), None),
            P(("dp", "expert"), None),
            P(("dp", "expert"), None),
            P(None, ("dp", "expert")),
            P(None, ("dp", "expert")),
            P(None, ("dp", "expert")),
            P("expert", None, "dp"),
            P("expert", None, "dp"),
            P("expert", None, "dp"),
            P("expert", "dp"),
            P("expert", "dp"),
            P("expert", "dp"),
            P("expert", "dp", None),
            P("expert", "dp", None),
            P("expert", "dp", None),
            P("expert", "dp"),
            P("expert", "dp"),
            P("expert", "dp"),
        ),
        check_vma=False,
    )
```

profile of v0, /device:TPU:0, one launch (start us, length us, event | category | flops | bytes accessed | tf_op | source)
XLA Modules:
  0.0 862.2 jit_solution(11749757161682119090)
XLA Ops:
  8.9 44.9 %all-gather.8.cloned.1.call-done = bf16[384,2304]{1,0:T(8,128)(2,1)} async-done(((bf16[24,2304]{1,0:T(8,128)(2,1)}), bf16[384,2304]{1,0:T(8,128)(2,1)}) %all-gather.8.cloned.1.call-update) | async-done | bytes 1769488 | tf_op jit(solution)/shard_map/all_gather | solution.py:139
  54.8 22.1 %all_gather.40 = bf16[384,768]{1,0:T(8,128)(2,1)} all-gather(bf16[24,768]{1,0:T(8,128)(2,1)S(1)} %convert_element_type.238), channel_id=1, replica_groups=mesh['dp'=2,'expert'=16] {'expert'}, dimensions={0}, use_global_device_ids=true | all-gather | bytes 626688 | tf_op jit(solution)/shard_map/all_gather | solution.py:140
  77.0 4.0 convert_element_type.243
  81.1 4.0 convert_element_type.246
  88.6 17.5 %all-gather = bf16[16,24,7]{1,2,0:T(8,128)(2,1)S(1)} all-gather(bf16[1,24,7]{1,2,0:T(8,128)(2,1)S(1)} %convert_bitcast_fusion.2), channel_id=1, replica_groups=mesh['dp'=2,'expert'=16] {'expert'}, dimensions={0}, use_global_device_ids=true | all-gather | bytes 5712 | tf_op jit(solution)/shard_map/all_gather | solution.py:142
  106.2 4.4 all_gather.37
  111.2 18.9 %all-gather.1 = bf16[16,24,16]{1,2,0:T(8,128)(2,1)S(1)} all-gather(bf16[1,24,16]{1,2,0:T(8,128)(2,1)S(1)} %convert_bitcast_fusion.1), channel_id=1, replica_groups=mesh['dp'=2,'expert'=16] {'expert'}, dimensions={0}, use_global_device_ids=true | all-gather | bytes 13056 | tf_op jit(solution)/shard_map/all_gather | solution.py:141
  130.2 4.5 all_gather.43
  136.2 4.9 fusion.102
  147.2 9.8 %multiply_reduce_fusion.1 = (f32[12,576]{1,0:T(8,128)S(1)}, f32[12,576,576]{1,2,0:T(8,128)}) fusion(bf16[576,12,64]{0,2,1:T(8,128)(2,1)} %bitcast.169, bf16[576,12,64]{0,2,1:T(8,128)(2,1)S(1)} %bitcast.165), kind=kOutput, calls=%fused_computation.7 | convolution fusion | flops 517563648 | bytes 17722368 | tf_op jit(solution)/shard_map/qhd,khd->hqk/dot_general | solution.py:181
  157.0 9.1 %fusion = f32[12,576]{1,0:T(8,128)S(1)} fusion(f32[12,576,576]{1,2,0:T(8,128)} %get-tuple-element.79, f32[12,576]{1,0:T(8,128)S(1)} %get-tuple-element.78), kind=kLoop, calls=%fused_computation.6 | loop fusion | flops 11937024 | bytes 15980544 | tf_op jit(solution)/shard_map/reduce_sum | solution.py:186
  166.2 8.8 %fusion.58 = bf16[12,64,576]{2,1,0:T(8,128)(2,1)} fusion(bf16[576,12,64]{0,2,1:T(8,128)(2,1)S(1)} %bitcast.172, f32[12,576,576]{1,2,0:T(8,128)} %get-tuple-element.79, f32[12,576]{1,0:T(8,128)S(1)} %fusion, f32[12,576]{1,0:T(8,128)S(1)} %get-tuple-element.78), kind=kOutput, calls=%fused_computation.99 | convolution fusion | flops 525975552 | bytes 17750016 | tf_op jit(solution)/shard_map/hqk,khd->qhd/dot_general | solution.py:190
  183.1 4.1 all-to-all-start.2
  192.3 16.4 %all-to-all-done.2 = bf16[16,36,768]{2,1,0:T(8,128)(2,1)S(1)} async-done(((bf16[16,36,768]{2,1,0:T(8,128)(2,1)}), bf16[16,36,768]{2,1,0:T(8,128)(2,1)S(1)}, u32[]{:S(2)}, u32[]{:S(2)}) %all-to-all-start.2) | async-done | bytes 884768 | tf_op jit(solution)/shard_map/all_to_all | solution.py:241
  208.6 6.5 all-to-all-start
  215.2 4.5 all_gather.45
  220.8 16.3 %all-to-all-done = bf16[16,36,768]{2,1,0:T(8,128)(2,1)} async-done(((bf16[16,36,768]{2,1,0:T(8,128)(2,1)}), bf16[16,36,768]{2,1,0:T(8,128)(2,1)}, u32[]{:S(2)}, u32[]{:S(2)}) %all-to-all-start) | async-done | bytes 884768 | tf_op jit(solution)/shard_map/all_to_all | solution.py:217
  239.2 8.4 fusion.30
  247.6 9.7 %all-gather.16.cloned.1.call-done = bf16[1,3072,768]{2,1,0:T(8,128)(2,1)} async-done(((bf16[1,1536,768]{2,1,0:T(8,128)(2,1)}), bf16[1,3072,768]{2,1,0:T(8,128)(2,1)}) %all-gather.16.cloned.1.call-update) | async-done | bytes 4718608 | tf_op jit(solution)/shard_map/all_gather | solution.py:157
  257.3 10.8 %fusion.125 = (bf16[3072]{0:T(1024)(128)(2,1)}, bf16[576,3072]{1,0:T(8,128)(2,1)S(1)}) fusion(f32[576,3072]{1,0:T(8,128)} %fusion.30, f32[3072]{0:T(1024)S(1)} %bitcast.189, bf16[576,768]{1,0:T(8,128)(2,1)} %reshape.280, bf16[1,3072,768]{2,1,0:T(8,128)(2,1)} %all-gather.16.cloned.1.call-done), kind=kOutput, calls=%fused_computation.211 | convolution fusion | flops 2756834304 | bytes 16238592 | tf_op jit(solution)/shard_map/dot_general | solution.py:48
  274.0 5.7 all-to-all-start.3
  279.7 4.5 all_gather.47
  284.2 8.8 %add_convert_fusion.1 = bf16[576,768]{1,0:T(8,128)(2,1)S(1)} fusion(bf16[1,3072,768]{2,1,0:T(8,128)(2,1)} %all-gather.16.cloned.1.call-done, f32[768]{0:T(1024)S(1)} %convert_reduce_fusion.1, f32[576,3072]{1,0:T(8,128)} %fusion.30, f32[3072]{0:T(1024)} %bitcast.190), kind=kOutput, calls=%fused_computation.94 | convolution fusion | flops 2736488448 | bytes 12696576 | tf_op jit(solution)/shard_map/dot_general | solution.py:38
  294.1 7.5 all-to-all-done.3
  301.6 6.6 all-to-all-start.1
  316.2 13.8 %all-to-all-done.1 = bf16[16,36,768]{2,1,0:T(8,128)(2,1)} async-done(((bf16[16,36,768]{2,1,0:T(8,128)(2,1)}), bf16[16,36,768]{2,1,0:T(8,128)(2,1)}, u32[]{:S(2)}, u32[]{:S(2)}) %all-to-all-start.1) | async-done | bytes 884768 | tf_op jit(solution)/shard_map/all_to_all | solution.py:226
  331.4 4.8 gather_fusion
  336.2 5.1 reshape.303
  341.3 9.1 %multiply_reduce_fusion.2 = (f32[576,2]{1,0:T(8,128)}, f32[576,768]{1,0:T(8,128)}) fusion(f32[576,2,768]{2,1,0:T(2,128)} %reshape.303, f32[576,768]{1,0:T(8,128)S(1)} %copy-done.15, f32[576,2]{1,0:T(8,128)} %copy.109), kind=kLoop, calls=%fused_computation.54 | loop fusion | flops 3095424 | bytes 7087104 | tf_op jit(solution)/shard_map/reduce_sum | solution.py:238
  366.9 11.9 %multiply_reduce_fusion = (f32[12,576]{1,0:T(8,128)S(1)}, f32[12,576,576]{1,2,0:T(8,128)}) fusion(f32[12,576,576]{1,2,0:T(8,128)} %get-tuple-element.79, f32[12,576]{1,0:T(8,128)S(1)} %copy-done.22, bf16[576,12,64]{0,2,1:T(8,128)(2,1)S(1)} %bitcast.167, bf16[576,12,64]{0,2,1:T(8,128)(2,1)} %bitcast.171), kind=kOutput, calls=%fused_computation.2 | convolution fusion | flops 525526272 | bytes 33675264 | tf_op jit(solution)/shard_map/qhd,khd->hqk/dot_general | solution.py:296
  378.8 12.7 %multiply_convert_fusion = bf16[12,576,576]{1,2,0:T(8,128)(2,1)S(1)} fusion(f32[12,576,576]{1,2,0:T(8,128)} %get-tuple-element.86, f32[12,576,576]{1,2,0:T(8,128)} %get-tuple-element.79, f32[12,576]{1,0:T(8,128)S(1)} %get-tuple-element.85, f32[12,576]{1,0:T(8,128)S(1)} %copy-done.22), kind=kLoop, calls=%fused_computation.1 | loop fusion | flops 19906560 | bytes 39868416 | tf_op jit(solution)/shard_map/convert_element_type | solution.py:306
  396.1 9.7 %bitcast_reduce_fusion = (bf16[12,64]{1,0:T(8,128)(2,1)S(1)}, bf16[12,64,576]{2,1,0:T(8,128)(2,1)S(1)}) fusion(bf16[576,12,64]{0,2,1:T(8,128)(2,1)S(1)} %bitcast.168, f32[12,576,576]{1,2,0:T(8,128)} %get-tuple-element.79, f32[12,576]{1,0:T(8,128)S(1)} %copy-done.22), kind=kOutput, calls=%fused_computation.107 | convolution fusion | flops 522435840 | bytes 17723904 | tf_op jit(solution)/shard_map/hqk,qhd->khd/dot_general | solution.py:299
  406.8 7.5 convolution_convert_fusion
  418.2 5.6 fusion.105
  430.2 10.5 %fusion.33 = bf16[1,3072,768]{2,1,0:T(8,128)(2,1)} fusion(bf16[576,768]{1,0:T(8,128)(2,1)} %reshape.280, f32[576,3072]{1,0:T(8,128)} %fusion.30, f32[3072]{0:T(1024)S(1)} %bitcast.191), kind=kOutput, calls=%fused_computation.53 | convolution fusion | flops 2737963008 | bytes 12693504 | tf_op jit(solution)/shard_map/dot_general | solution.py:42
  440.8 8.3 fusion.32
  449.2 13.9 %reduce-scatter.21.cloned.1.call-done = bf16[384,2304]{1,0:T(8,128)(2,1)} async-done(((bf16[768,2304]{1,0:T(8,128)(2,1)}), bf16[384,2304]{1,0:T(8,128)(2,1)}) %reduce-scatter.21.cloned.1.call-update) | async-done | bytes 1769488 | tf_op jit(solution)/shard_map/reduce_scatter | solution.py:342
  464.4 12.5 %reduce-scatter.39.cloned.1.call-done = bf16[384,1]{1,0:T(8,128)(2,1)} async-done(((bf16[768,1]{1,0:T(8,128)(2,1)}), bf16[384,1]{1,0:T(8,128)(2,1)}) %reduce-scatter.39.cloned.1.call-update) | async-done | bytes 784
  478.5 18.7 %reduce-scatter.37.cloned.1.call-done = bf16[1536,1]{1,0:T(8,128)(2,1)} async-done(((bf16[3072,1]{1,0:T(8,128)(2,1)}), bf16[1536,1]{1,0:T(8,128)(2,1)}) %reduce-scatter.37.cloned.1.call-update) | async-done | bytes 3088
  499.0 11.9 %reduce-scatter.35.cloned.1.call-done = bf16[384,7]{1,0:T(8,128)(2,1)} async-done(((bf16[768,7]{1,0:T(8,128)(2,1)}), bf16[384,7]{1,0:T(8,128)(2,1)}) %reduce-scatter.35.cloned.1.call-update) | async-done | bytes 5392
  511.9 12.9 %reduce-scatter.33.cloned.1.call-done = bf16[384,16]{1,0:T(8,128)(2,1)} async-done(((bf16[768,16]{1,0:T(8,128)(2,1)}), bf16[384,16]{1,0:T(8,128)(2,1)}) %reduce-scatter.33.cloned.1.call-update) | async-done | bytes 12304
  525.8 61.2 %all-reduce.2 = (bf16[384,16]{0,1:T(8,128)(2,1)S(1)}, bf16[7,384]{1,0:T(8,128)(2,1)S(1)}) all-reduce(bf16[384,16]{0,1:T(8,128)(2,1)S(1)} %copy.121, bf16[7,384]{1,0:T(8,128)(2,1)S(1)} %copy.125), channel_id=7, replica_groups=mesh['dp'=2,'expert'=16] {'expert'}, use_global_device_ids=true, to_apply=%region_28.29.clone | all-reduce | flops 8832 | bytes 35328
  589.8 55.7 %reduce-scatter.31.cloned.1.call-done = bf16[1,1536,768]{2,1,0:T(8,128)(2,1)} async-done(((bf16[1,3072,768]{2,1,0:T(8,128)(2,1)}), bf16[1,1536,768]{2,1,0:T(8,128)(2,1)}) %reduce-scatter.31.cloned.1.call-update) | async-done | bytes 2359312 | tf_op jit(solution)/shard_map/reduce_scatter | solution.py:263
  649.0 59.4 %reduce-scatter.29.cloned.1.call-done = bf16[1,768,1536]{2,1,0:T(8,128)(2,1)} async-done(((bf16[1,768,3072]{2,1,0:T(8,128)(2,1)}), bf16[1,768,1536]{2,1,0:T(8,128)(2,1)}) %reduce-scatter.29.cloned.1.call-update) | async-done | bytes 2359312 | tf_op jit(solution)/shard_map/reduce_scatter | solution.py:257
  711.8 60.4 %reduce-scatter.23.cloned.1.call-done = bf16[24,2304]{1,0:T(8,128)(2,1)} async-done(((bf16[384,2304]{1,0:T(8,128)(2,1)}), bf16[24,2304]{1,0:T(8,128)(2,1)}) %reduce-scatter.23.cloned.1.call-update) | async-done | bytes 110608 | tf_op jit(solution)/shard_map/reduce_scatter | solution.py:356
  782.9 40.0 %psum.7 = f32[]{:T(128)} all-reduce(f32[]{:T(128)S(6)} %add.376), channel_id=1, replica_groups=mesh['dp'=2,'expert'=16] {'dp','expert'}, use_global_device_ids=true, to_apply=%region_50.51 | all-reduce | flops 1 | bytes 8 | tf_op jit(solution)/shard_map/psum | solution.py:373
  832.8 11.7 %multiply_subtract_fusion = (f32[1,1536,768]{2,1,0:T(8,128)}, f32[1,1536,768]{2,1,0:T(8,128)}, f32[1,1536,768]{2,1,0:T(8,128)}) fusion(f32[1,1536,768]{2,1,0:T(8,128)} %param.50, f32[]{:T(128)S(6)} %div.205, bf16[1,1536,768]{2,1,0:T(8,128)(2,1)} %reduce-scatter.31.cloned.1.call-done, f32[1,1536,768]{2,1,0:T(8,128)} %param.51, f32[1,1536,768]{2,1,0:T(8,128)} %param.52), kind=kLoop, calls=%fused_computation.50 | loop fusion | flops 20054016 | bytes 30670852 | tf_op jit(solution)/shard_map/sub | solution.py:90
  845.5 8.8 %multiply_subtract_fusion.1 = (f32[1,768,1536]{2,1,0:T(8,128)}, f32[1,768,1536]{2,1,0:T(8,128)}, f32[1,768,1536]{2,1,0:T(8,128)}) fusion(f32[1,768,1536]{2,1,0:T(8,128)S(1)} %bitcast.164, f32[]{:T(128)S(6)} %div.205, bf16[1,768,1536]{2,1,0:T(8,128)(2,1)S(1)} %copy-done.4, f32[1,768,1536]{2,1,0:T(8,128)} %param.45, f32[1,768,1536]{2,1,0:T(8,128)} %param.46), kind=kLoop, calls=%fused_computation.51 | loop fusion | flops 20054016 | bytes 30670852 | tf_op jit(solution)/shard_map/sub | solution.py:90
  (310 shorter events, 110.3 us)
Async XLA Ops:
  7.2 46.7 %all-gather.8.cloned.1.call-start = ((), (), s32[]{:S(2)}) async-start(), calls=%async_computation.14 | async-start | bytes 1880064 | tf_op jit(solution)/shard_map/all_gather | solution.py:139
  8.9 127.3 %all-gather.10.cloned.1.call-start = ((), (), s32[]{:S(2)}) async-start(), calls=%async_computation.15 | async-start | bytes 5308416 | tf_op jit(solution)/shard_map/all_gather | solution.py:145
  53.9 121.1 %all-gather.12.cloned.1.call-start = ((), (), s32[]{:S(2)}) async-start(), calls=%async_computation.16 | async-start | bytes 1769472 | tf_op jit(solution)/shard_map/all_gather | solution.py:146
  76.9 162.3 %all-gather.14.cloned.1.call-start = ((), (), s32[]{:S(2)}) async-start(), calls=%async_computation.17 | async-start | bytes 7077888 | tf_op jit(solution)/shard_map/all_gather | solution.py:155
  81.1 176.2 %all-gather.16.cloned.1.call-start = ((), (), s32[]{:S(2)}) async-start(), calls=%async_computation.18 | async-start | bytes 7077888 | tf_op jit(solution)/shard_map/all_gather | solution.py:157
  86.8 49.4 %copy-start.36 = (f32[576]{0:T(1024)}, f32[576]{0:T(1024)S(1)}, u32[]{:S(2)}) copy-start(f32[576]{0:T(1024)S(1)} %broadcast_multiply_fusion.1) | copy-start | bytes 6916
  87.8 48.4 %copy-start.48 = (f32[576]{0:T(1024)}, f32[576]{0:T(1024)S(1)}, u32[]{:S(2)}) copy-start(f32[576]{0:T(1024)S(1)} %fusion.94) | copy-start | bytes 6916
  88.0 48.2 %copy-start.40 = (pred[2,576]{1,0:T(4,128)(4,1)}, pred[2,576]{1,0:T(4,128)(4,1)S(1)}, u32[]{:S(2)}) copy-start(pred[2,576]{1,0:T(4,128)(4,1)S(1)} %lt.32) | copy-start | bytes 3460
  88.6 47.6 %copy-start.44 = (s32[576,2]{0,1:T(2,128)}, s32[576,2]{0,1:T(2,128)S(1)}, u32[]{:S(2)}) copy-start(s32[576,2]{0,1:T(2,128)S(1)} %get-tuple-element.74) | copy-start | bytes 13828
  111.2 25.0 %copy-start.46 = (f32[768]{0:T(1024)}, f32[768]{0:T(1024)S(1)}, u32[]{:S(2)}) copy-start(f32[768]{0:T(1024)S(1)} %get-tuple-element.42) | copy-start | bytes 9220
  111.2 25.1 %copy-start.67 = (f32[768]{0:T(1024)}, f32[768]{0:T(1024)S(1)}, u32[]{:S(2)}) copy-start(f32[768]{0:T(1024)S(1)} %get-tuple-element.41) | copy-start | bytes 9220
  111.2 66.9 %copy-start.34 = (f32[768]{0:T(1024)}, f32[768]{0:T(1024)S(1)}, u32[]{:S(2)}) copy-start(f32[768]{0:T(1024)S(1)} %get-tuple-element.36) | copy-start | bytes 9220
  144.6 12.3 %copy-start.2 = (bf16[576,768]{0,1:T(8,128)(2,1)}, bf16[576,768]{0,1:T(8,128)(2,1)S(1)}, u32[]{:S(2)}) copy-start(bf16[576,768]{0,1:T(8,128)(2,1)S(1)} %copy.106) | copy-start | bytes 2654212
  183.1 32.0 %copy-start.56 = (f32[1,1536]{1,0:T(1,128)S(1)}, f32[1,1536]{1,0:T(1,128)}, u32[]{:S(2)}) copy-start(f32[1,1536]{1,0:T(1,128)} %param.47) | copy-start | bytes 18436
  183.1 25.5 %all-to-all-start.2 = ((bf16[16,36,768]{2,1,0:T(8,128)(2,1)}), bf16[16,36,768]{2,1,0:T(8,128)(2,1)S(1)}, u32[]{:S(2)}, u32[]{:S(2)}) async-start(bf16[16,36,768]{2,1,0:T(8,128)(2,1)} %reshape.279), calls=%async_computation.2 | async-start | bytes 1966080 | tf_op jit(solution)/shard_map/all_to_all | solution.py:241
  208.6 39.0 %copy-start.5 = (bf16[16,36,768]{2,1,0:T(8,128)(2,1)}, bf16[16,36,768]{2,1,0:T(8,128)(2,1)S(1)}, u32[]{:S(2)}) copy-start(bf16[16,36,768]{2,1,0:T(8,128)(2,1)S(1)} %all-to-all-done.2) | copy-start | bytes 2654212
  208.6 28.5 %all-to-all-start = ((bf16[16,36,768]{2,1,0:T(8,128)(2,1)}), bf16[16,36,768]{2,1,0:T(8,128)(2,1)}, u32[]{:S(2)}, u32[]{:S(2)}) async-start(bf16[16,36,768]{2,1,0:T(8,128)(2,1)} %reshape.275), calls=%async_computation | async-start | bytes 1966080 | tf_op jit(solution)/shard_map/all_to_all | solution.py:217
  219.7 37.6 %copy-start.61 = (f32[1,3072]{1,0:T(1,128)}, f32[1,3072]{1,0:T(1,128)S(1)}, u32[]{:S(2)}) copy-start(f32[1,3072]{1,0:T(1,128)S(1)} %add.417) | copy-start | bytes 36868
  257.3 12.6 %copy-start.72 = (bf16[1,768,3072]{2,1,0:T(8,128)(2,1)S(1)}, bf16[1,768,3072]{2,1,0:T(8,128)(2,1)}, u32[]{:S(2)}) copy-start(bf16[1,768,3072]{2,1,0:T(8,128)(2,1)} %all-gather.14.cloned.1.call-done) | copy-start | bytes 14155780
  274.0 27.6 %all-to-all-start.3 = ((bf16[16,36,768]{2,1,0:T(8,128)(2,1)}), bf16[16,36,768]{2,1,0:T(8,128)(2,1)}, u32[]{:S(2)}, u32[]{:S(2)}) async-start(bf16[16,36,768]{2,1,0:T(8,128)(2,1)} %reshape.281), calls=%async_computation.3 | async-start | bytes 1966080 | tf_op jit(solution)/shard_map/all_to_all | solution.py:270
  293.0 16.3 %copy-start.11 = (bf16[1,576,768]{2,1,0:T(8,128)(2,1)S(1)}, bf16[1,576,768]{2,1,0:T(8,128)(2,1)}, u32[]{:S(2)}) copy-start(bf16[1,576,768]{2,1,0:T(8,128)(2,1)} %param.29) | copy-start | bytes 2654212
  294.1 16.5 %copy-start.43 = (f32[576,2]{0,1:T(2,128)S(1)}, f32[576,2]{0,1:T(2,128)}, u32[]{:S(2)}) copy-start(f32[576,2]{0,1:T(2,128)} %copy-done.42) | copy-start | bytes 13828
  294.1 17.4 %copy-start.39 = (f32[576]{0:T(1024)S(1)}, f32[576]{0:T(1024)}, u32[]{:S(2)}) copy-start(f32[576]{0:T(1024)} %copy-done.38) | copy-start | bytes 6916
  294.1 18.0 %copy-start.25 = (f32[12,576]{1,0:T(8,128)S(1)}, f32[12,576]{1,0:T(8,128)}, u32[]{:S(2)}) copy-start(f32[12,576]{1,0:T(8,128)} %copy-done.24) | copy-start | bytes 82948
  294.1 18.0 %copy-start.32 = (f32[12,576]{1,0:T(8,128)S(1)}, f32[12,576]{1,0:T(8,128)}, u32[]{:S(2)}) copy-start(f32[12,576]{1,0:T(8,128)} %copy-done.31) | copy-start | bytes 82948
  294.1 19.9 %copy-start.27 = (pred[576,576]{1,0:T(8,128)(4,1)S(1)}, pred[576,576]{1,0:T(8,128)(4,1)}, u32[]{:S(2)}) copy-start(pred[576,576]{1,0:T(8,128)(4,1)} %fusion.35) | copy-start | bytes 995332
  301.6 28.5 %all-to-all-start.1 = ((bf16[16,36,768]{2,1,0:T(8,128)(2,1)}), bf16[16,36,768]{2,1,0:T(8,128)(2,1)}, u32[]{:S(2)}, u32[]{:S(2)}) async-start(bf16[16,36,768]{2,1,0:T(8,128)(2,1)} %reshape.277), calls=%async_computation.1 | async-start | bytes 1966080 | tf_op jit(solution)/shard_map/all_to_all | solution.py:226
  308.1 121.3 %reduce-scatter.25.cloned.1.call-start = ((), (), s32[]{:S(2)}) async-start(), calls=%async_computation.21 | async-start | bytes 1769472 | tf_op jit(solution)/shard_map/reduce_scatter | solution.py:345
  366.7 96.5 %reduce-scatter.21.cloned.1.call-start = ((), (), s32[]{:S(2)}) async-start(), calls=%async_computation.19 | async-start | bytes 5308416 | tf_op jit(solution)/shard_map/reduce_scatter | solution.py:342
  378.8 12.7 %copy-start.8 = (bf16[576,768]{0,1:T(8,128)(2,1)S(1)}, bf16[576,768]{0,1:T(8,128)(2,1)}, u32[]{:S(2)}) copy-start(bf16[576,768]{0,1:T(8,128)(2,1)} %copy.105) | copy-start | bytes 2654212
  414.3 62.6 %reduce-scatter.39.cloned.1.call-start = ((), (), s32[]{:S(2)}) async-start(), calls=%async_computation.28 | async-start | bytes 294912
  416.6 80.6 %reduce-scatter.37.cloned.1.call-start = ((), (), s32[]{:S(2)}) async-start(), calls=%async_computation.27 | async-start | bytes 1179648
  418.1 92.9 %reduce-scatter.35.cloned.1.call-start = ((), (), s32[]{:S(2)}) async-start(), calls=%async_computation.26 | async-start | bytes 294912
  427.1 97.8 %reduce-scatter.33.cloned.1.call-start = ((), (), s32[]{:S(2)}) async-start(), calls=%async_computation.25 | async-start | bytes 294912
  429.4 159.0 %reduce-scatter.27.cloned.1.call-start = ((), (), s32[]{:S(2)}) async-start(), calls=%async_computation.22 | async-start | bytes 626688 | tf_op jit(solution)/shard_map/reduce_scatter | solution.py:359
  430.0 215.5 %reduce-scatter.31.cloned.1.call-start = ((), (), s32[]{:S(2)}) async-start(), calls=%async_computation.24 | async-start | bytes 7077888 | tf_op jit(solution)/shard_map/reduce_scatter | solution.py:263
  440.7 267.6 %reduce-scatter.29.cloned.1.call-start = ((), (), s32[]{:S(2)}) async-start(), calls=%async_computation.23 | async-start | bytes 7077888 | tf_op jit(solution)/shard_map/reduce_scatter | solution.py:257
  449.1 14.1 %copy-start.74 = (u32[32]{0:T(128)S(1)}, u32[32]{0:T(128)}, u32[]{:S(2)}) copy-start(u32[32]{0:T(128)} %constant.179) | copy-start | bytes 388
  449.2 323.1 %reduce-scatter.23.cloned.1.call-start = ((), (), s32[]{:S(2)}) async-start(), calls=%async_computation.20 | async-start | bytes 1880064 | tf_op jit(solution)/shard_map/reduce_scatter | solution.py:356
  477.9 34.0 %copy-start.60 = (bf16[1,384]{1,0:T(2,128)(2,1)}, bf16[1,384]{1,0:T(2,128)(2,1)S(1)}, u32[]{:S(2)}) copy-start(bf16[1,384]{1,0:T(2,128)(2,1)S(1)} %copy.131) | copy-start | bytes 2308
  587.0 58.5 %copy-start.66 = (bf16[384,16]{0,1:T(8,128)(2,1)}, bf16[384,16]{0,1:T(8,128)(2,1)S(1)}, u32[]{:S(2)}) copy-start(bf16[384,16]{0,1:T(8,128)(2,1)S(1)} %get-tuple-element.43) | copy-start | bytes 36868
  587.0 58.5 %copy-start.70 = (bf16[7,384]{1,0:T(8,128)(2,1)}, bf16[7,384]{1,0:T(8,128)(2,1)S(1)}, u32[]{:S(2)}) copy-start(bf16[7,384]{1,0:T(8,128)(2,1)S(1)} %get-tuple-element.44) | copy-start | bytes 16132
  649.0 175.9 %copy-start.59 = (f32[7,24]{1,0:T(8,128)S(1)}, f32[7,24]{1,0:T(8,128)}, u32[]{:S(2)}) copy-start(f32[7,24]{1,0:T(8,128)} %param.41) | copy-start | bytes 2020
  649.0 177.3 %copy-start.55 = (f32[24,16]{0,1:T(8,128)S(1)}, f32[24,16]{0,1:T(8,128)}, u32[]{:S(2)}) copy-start(f32[24,16]{0,1:T(8,128)} %param.38) | copy-start | bytes 4612
  649.0 181.8 %copy-start.21 = (f32[24,2304]{1,0:T(8,128)S(1)}, f32[24,2304]{1,0:T(8,128)}, u32[]{:S(2)}) copy-start(f32[24,2304]{1,0:T(8,128)} %param.32) | copy-start | bytes 663556
  772.3 58.5 %copy-start.23 = (bf16[24,2304]{1,0:T(8,128)(2,1)S(1)}, bf16[24,2304]{1,0:T(8,128)(2,1)}, u32[]{:S(2)}) copy-start(bf16[24,2304]{1,0:T(8,128)(2,1)} %reduce-scatter.23.cloned.1.call-done) | copy-start | bytes 331780
  779.1 65.4 %slice-start = ((s8[4718592]{0:T(1024)(128)(4,1)}), s8[524288]{0:T(1024)(128)(4,1)S(1)}, s32[]{:S(2)}) async-start(s8[4718592]{0:T(1024)(128)(4,1)} %bitcast.163), calls=%async_computation.29 | async-start | bytes 1048576
  832.8 12.8 %copy-start.4 = (bf16[1,768,1536]{2,1,0:T(8,128)(2,1)S(1)}, bf16[1,768,1536]{2,1,0:T(8,128)(2,1)}, u32[]{:S(2)}) copy-start(bf16[1,768,1536]{2,1,0:T(8,128)(2,1)} %reduce-scatter.29.cloned.1.call-done) | copy-start | bytes 7077892
  (49 other events, 274.3 us)
Sparse Core Ops, SparseCore 0:
  10.8 43.0 all-gather.7
  55.4 47.9 all-gather.9
  105.0 22.7 all-gather.11
  129.8 62.6 all-gather.13
  194.4 62.7 all-gather.15
  366.8 22.6 reduce-scatter.24
  414.4 48.6 reduce-scatter.20
  465.9 10.9 reduce-scatter.38
  479.8 17.4 reduce-scatter.36
  500.0 10.9 reduce-scatter.34
  513.9 10.9 reduce-scatter.32
  528.7 54.8 reduce-scatter.26
  586.4 59.0 reduce-scatter.30
  648.3 59.9 reduce-scatter.28
  712.0 60.2 reduce-scatter.22
where the time goes:
time: 869 us; the launch traced here: 862 us
  waiting for transfers between devices  355 us (41%)
  blocking collectives  178 us (20%)
  matrix products  132 us (15%)
  other arithmetic  103 us (12%)
  local copies, waits for them, and re-layouts  47.8 us (6%)
  starting transfers between devices  23.8 us (3%)
  between operations  22.9 us (3%)
    unnamed x1, blocking collectives  61.2 us
    reduce_scatter x1, waiting for transfers between devices, shards(): lax.psum_scatter(partial_grads[0].astype(jnp.bfloat16), 'expert', scatter...  60.4 us
    reduce_scatter x1, waiting for transfers between devices, shards(): lax.psum_scatter(inner_grad[None].astype(jnp.bfloat16), 'dp', scatter_dim...  59.4 us
    unnamed x19, waiting for transfers between devices  56.8 us
    reduce_scatter x1, waiting for transfers between devices, shards(): lax.psum_scatter(outer_grad[None].astype(jnp.bfloat16), 'dp', scatter_dim...  55.7 us
    all_gather x1, waiting for transfers between devices, shards(): lax.all_gather(dense_shards[0], 'expert', axis=0, tiled=True)  44.9 us
    psum x1, blocking collectives, shards(): square_total = lax.psum(local_square, ('dp', 'expert'))  40 us
    dot_general x6, matrix products, rows_product(): lax.dot_general(left, right, (((0,), (0,)), ((), ())), preferred_element_...  32.1 us
  transfers between devices with their start and end apart: 19, of which 14 were waited for; matrix products, arithmetic and copies ran while one was open for 22% of the time, Pallas kernels for 0%

commit v1 on v0

--- a/solution.py
+++ b/solution.py
@@ -1,6 +1,10 @@
+import functools
+
 import jax
 import jax.numpy as jnp
 from jax import lax
+from jax.experimental import pallas as pl
+from jax.experimental.pallas import tpu as pltpu
 from jax.sharding import PartitionSpec as P
 
 HEADS = 12
@@ -434,9 +438,628 @@
     )
 
 
+MESH = pl.DeviceIdType.MESH
+ANY = pl.BlockSpec(memory_space=pl.ANY)
+VMEM = pl.BlockSpec(memory_space=pltpu.VMEM)
+
+
+class Place:
+    def __init__(self, dp, experts):
+        self.dp, self.experts = dp, experts
+        self.ys = 2
+        self.zs = experts // 4
+        self.a = lax.axis_index("dp")
+        self.e = lax.axis_index("expert")
+        self.core = lax.rem(self.e, 2)
+        self.y = lax.rem(lax.div(self.e, 2), self.ys)
+        self.z = lax.div(self.e, 2 * self.ys)
+
+    def chip_of(self, core, dz, s2, s3):
+        zz = lax.rem(self.z + dz, self.zs)
+        if s2 == s3:
+            fa = fy = s2
+        elif s2:
+            fa, fy = core, 1 - core
+        else:
+            fa, fy = 1 - core, core
+        aa = lax.rem(self.a + fa, 2)
+        yy = lax.rem(self.y + fy, 2)
+        return aa, zz, yy
+
+    def device(self, core, dz, s2, s3, own_core=None):
+        aa, zz, yy = self.chip_of(core, dz, s2, s3)
+        c = core if own_core is None else own_core
+        return (aa, (zz * self.ys + yy) * 2 + c)
+
+    def flat(self, dev):
+        return dev[0] * self.experts + dev[1]
+
+    def chip(self, core, dz, s2, s3):
+        aa, zz, yy = self.chip_of(core, dz, s2, s3)
+        return (aa * self.zs + zz) * self.ys + yy
+
+
+def remote(src, dst, send, recv, dev):
+    return pltpu.make_async_remote_copy(src_ref=src, dst_ref=dst, send_sem=send, recv_sem=recv, device_id=dev, device_id_type=MESH)
+
+
+def greet(devices):
+    barrier = pltpu.get_barrier_semaphore()
+    for dev in devices:
+        pl.semaphore_signal(barrier, inc=1, device_id=dev, device_id_type=MESH)
+    pl.semaphore_wait(barrier, len(devices))
+
+
+def split_index(k, zs):
+    return k % zs, (k // zs) % 2, k // (2 * zs)
+
+
+def gather_kernel(dp, experts, in_ref, out_ref, send, recv, csend, crecv, own):
+    p = Place(dp, experts)
+    zs = p.zs
+    c = p.core
+    n = 4 * zs
+    partner = (p.a, p.e + 1 - 2 * c)
+    peers = [p.device(c, dz, 0, 0) for dz in range(1, zs)]
+    second = p.device(c, 0, 1, 0)
+    third = p.device(c, 0, 0, 1)
+    me = p.flat((p.a, p.e))
+    mine = pltpu.make_async_copy(in_ref, out_ref.at[me], own)
+    mine.start()
+    greet(peers + [second, third, partner])
+    pending = []
+
+    def block(k):
+        if k == 0:
+            return me, in_ref
+        dz, s2, s3 = split_index(k, zs)
+        at = p.flat(p.device(c, (zs - dz) % zs, s2, s3))
+        return at, out_ref.at[at]
+
+    def push(k, slot, dev):
+        at, src = block(k)
+        cp = remote(src, out_ref.at[at], send.at[slot], recv.at[slot], dev)
+        cp.start()
+        pending.append(cp)
+
+    def hand(k):
+        at, src = block(k)
+        cp = remote(src, out_ref.at[at], csend.at[k], crecv.at[k], partner)
+        cp.start()
+        pending.append(cp)
+
+    def arrived(k):
+        at, _ = block(k)
+        remote(in_ref, out_ref.at[at], send.at[k], recv.at[k], partner).wait_recv()
+
+    for dz in range(1, zs):
+        push(0, dz, peers[dz - 1])
+    push(0, zs, second)
+    push(0, 2 * zs, third)
+    hand(0)
+    for k in range(1, zs):
+        arrived(k)
+        push(k, zs + k, second)
+        push(k, 2 * zs + k, third)
+        hand(k)
+    for k in range(zs, 2 * zs):
+        arrived(k)
+        push(k, 2 * zs + k, third)
+        hand(k)
+    for k in range(2 * zs, 4 * zs):
+        arrived(k)
+        hand(k)
+    for k in range(n):
+        dz, s2, s3 = split_index(k, zs)
+        at = p.flat(p.device(1 - c, (zs - dz) % zs, s2, s3))
+        remote(in_ref, out_ref.at[at], csend.at[k], crecv.at[k], partner).wait_recv()
+    for cp in pending:
+        cp.wait_send()
+    mine.wait()
+
+
+def gather_blocks(block, dp, experts, cid):
+    n = dp * experts
+    return pl.pallas_call(
+        functools.partial(gather_kernel, dp, experts),
+        out_shape=jax.ShapeDtypeStruct((n,) + block.shape, block.dtype),
+        in_specs=[ANY],
+        out_specs=ANY,
+        scratch_shapes=[
+            pltpu.SemaphoreType.DMA((n // 2,)),
+            pltpu.SemaphoreType.DMA((n // 2,)),
+            pltpu.SemaphoreType.DMA((n // 2,)),
+            pltpu.SemaphoreType.DMA((n // 2,)),
+            pltpu.SemaphoreType.DMA,
+        ],
+        compiler_params=pltpu.CompilerParams(collective_id=cid, has_side_effects=True),
+        name="gather_dense",
+    )(block)
+
+
+def dispatch_kernel(dp, experts, *refs):
+    m = (len(refs) - 5) // 2
+    ins, outs = refs[:m], refs[m : 2 * m]
+    send, recv, xsend, xrecv, own = refs[2 * m :]
+    a = lax.axis_index("dp")
+    e = lax.axis_index("expert")
+    across = (1 - a, e)
+    others = [(a, lax.rem(e + j, experts)) for j in range(1, experts)]
+    locals_ = []
+    for i in range(m):
+        cp = pltpu.make_async_copy(ins[i].at[e], outs[i].at[a, e], own.at[i])
+        cp.start()
+        locals_.append(cp)
+    greet(others + [across])
+    pending = []
+    for i in range(m):
+        cp = remote(ins[i].at[e], outs[i].at[a, e], xsend.at[i, 0], xrecv.at[i, 0], across)
+        cp.start()
+        pending.append(cp)
+        for j in range(1, experts):
+            dev = others[j - 1]
+            cp = remote(ins[i].at[dev[1]], outs[i].at[a, e], send.at[i, j], recv.at[i, j], dev)
+            cp.start()
+            pending.append(cp)
+    for i in range(m):
+        for j in range(1, experts):
+            src = lax.rem(e + experts - j, experts)
+            here = outs[i].at[a, src]
+            remote(here, here, send.at[i, j], recv.at[i, j], across).wait_recv()
+            cp = remote(here, here, xsend.at[i, j], xrecv.at[i, j], across)
+            cp.start()
+            pending.append(cp)
+    for i in range(m):
+        for j in range(experts):
+            src = lax.rem(e + experts - j, experts)
+            there = outs[i].at[1 - a, src]
+            remote(there, there, xsend.at[i, j], xrecv.at[i, j], across).wait_recv()
+    for cp in pending:
+        cp.wait_send()
+    for cp in locals_:
+        cp.wait()
+
+
+def dispatch(arrays, dp, experts, cid):
+    m = len(arrays)
+    shape = (dp,) + arrays[0].shape
+    return pl.pallas_call(
+        functools.partial(dispatch_kernel, dp, experts),
+        out_shape=[jax.ShapeDtypeStruct(shape, x.dtype) for x in arrays],
+        in_specs=[ANY] * m,
+        out_specs=[ANY] * m,
+        scratch_shapes=[pltpu.SemaphoreType.DMA((m, experts)) for _ in range(4)] + [pltpu.SemaphoreType.DMA((m,))],
+        compiler_params=pltpu.CompilerParams(collective_id=cid, has_side_effects=True),
+        name="dispatch_rows",
+    )(*arrays)
+
+
+def return_kernel(dp, experts, *refs):
+    m = (len(refs) - 7) // 2
+    ins, outs = refs[:m], refs[m : 2 * m]
+    mine, theirs, send, recv, xsend, xrecv, load = refs[2 * m :]
+    a = lax.axis_index("dp")
+    e = lax.axis_index("expert")
+    across = (1 - a, e)
+    others = [(a, lax.rem(e + j, experts)) for j in range(1, experts)]
+    pending = []
+    loads = []
+    for i in range(m):
+        for j in range(experts):
+            dst = lax.rem(e + j, experts)
+            cp = pltpu.make_async_copy(ins[i].at[a, dst], mine.at[i, j], load.at[i, j])
+            cp.start()
+            loads.append(cp)
+    greet(others + [across])
+    order = list(range(1, experts)) + [0]
+    for i in range(m):
+        for j in order:
+            dst = lax.rem(e + j, experts)
+            cp = remote(ins[i].at[1 - a, dst], theirs.at[i, j], xsend.at[i, j], xrecv.at[i, j], across)
+            cp.start()
+            pending.append(cp)
+    for i in range(m):
+        for j in order:
+            loads[i * experts + j].wait()
+            remote(theirs.at[i, j], theirs.at[i, j], xsend.at[i, j], xrecv.at[i, j], across).wait_recv()
+            mine[i, j] = (mine[i, j].astype(jnp.float32) + theirs[i, j].astype(jnp.float32)).astype(mine.dtype)
+            if j == 0:
+                last = pltpu.make_async_copy(mine.at[i, j], outs[i].at[e], load.at[i, j])
+                last.start()
+                loads[i * experts + j] = last
+            else:
+                cp = remote(mine.at[i, j], outs[i].at[e], send.at[i, j], recv.at[i, j], others[j - 1])
+                cp.start()
+                pending.append(cp)
+    for i in range(m):
+        for j in range(1, experts):
+            src = lax.rem(e + experts - j, experts)
+            remote(outs[i].at[src], outs[i].at[src], send.at[i, j], recv.at[i, j], across).wait_recv()
+        loads[i * experts].wait()
+    for cp in pending:
+        cp.wait_send()
+
+
+def give_back(arrays, dp, experts, cid):
+    m = len(arrays)
+    shape = arrays[0].shape[1:]
+    return pl.pallas_call(
+        functools.partial(return_kernel, dp, experts),
+        out_shape=[jax.ShapeDtypeStruct(shape, x.dtype) for x in arrays],
+        in_specs=[ANY] * m,
+        out_specs=[ANY] * m,
+        scratch_shapes=[pltpu.VMEM((m,) + shape, arrays[0].dtype)] * 2
+        + [pltpu.SemaphoreType.DMA((m, experts)) for _ in range(5)],
+        compiler_params=pltpu.CompilerParams(collective_id=cid, has_side_effects=True, vmem_limit_bytes=32 * 1024 * 1024),
+        name="return_rows",
+    )(*arrays)
+
+
+def reduce_kernel(dp, experts, grad_ref, part_ref, out_ref, total_ref, own, rc, r3, r2, rz, fin, row, tiles,
+                  load, csend, crecv, send, recv, fsend, frecv, nsend, nrecv):
+    p = Place(dp, experts)
+    zs = p.zs
+    c = p.core
+    n = 4 * zs
+    world = dp * experts
+    half = own.shape[2]
+    deep = own.shape[1] // 2
+    partner = (p.a, p.e + 1 - 2 * c)
+    second = p.device(c, 0, 1, 0)
+    third = p.device(c, 0, 0, 1)
+    me = p.flat((p.a, p.e))
+    everyone = []
+    for j in range(1, world):
+        other = lax.rem(me + j, world)
+        everyone.append((lax.div(other, experts), lax.rem(other, experts)))
+    mycols = pl.ds(pl.multiple_of(c * half, 128), half)
+    hiscols = pl.ds(pl.multiple_of((1 - c) * half, 128), half)
+    order = list(range(2 * zs, n)) + list(range(zs, 2 * zs)) + list(range(1, zs)) + [0]
+    loads = {}
+    for k in order:
+        loads[k] = pltpu.make_async_copy(grad_ref.at[p.chip(c, *split_index(k, zs)), :, mycols], own.at[k], load.at[k])
+        loads[k].start()
+    greet(everyone)
+    pending = []
+
+    def push(src, dst, ss, rs, dev):
+        cp = remote(src, dst, ss, rs, dev)
+        cp.start()
+        pending.append(cp)
+
+    for k in order:
+        push(grad_ref.at[p.chip(1 - c, *split_index(k, zs)), :, hiscols], rc.at[k], csend.at[k], crecv.at[k], partner)
+
+    def got(ref, sem):
+        remote(ref, ref, sem, sem, partner).wait_recv()
+
+    for k in order:
+        loads[k].wait()
+        got(rc.at[k], crecv.at[k])
+        total = own[k].astype(jnp.float32) + rc[k].astype(jnp.float32)
+        if k < 2 * zs:
+            got(r3.at[k], recv.at[2 * zs + k])
+            total = total + r3[k].astype(jnp.float32)
+        if k < zs:
+            got(r2.at[k], recv.at[zs + k])
+            total = total + r2[k].astype(jnp.float32)
+        if k >= 1:
+            own[k] = total.astype(own.dtype)
+        if k >= 2 * zs:
+            push(own.at[k], r3.at[k - 2 * zs], send.at[k], recv.at[k], third)
+        elif k >= zs:
+            push(own.at[k], r2.at[k - zs], send.at[k], recv.at[k], second)
+        elif k >= 1:
+            push(own.at[k], rz.at[k - 1], send.at[k], recv.at[k], p.device(c, k, 0, 0))
+        else:
+            for j in range(1, zs):
+                got(rz.at[j - 1], recv.at[j])
+                total = total + rz[j - 1].astype(jnp.float32)
+            fin[...] = total
+    his = pl.ds(pl.multiple_of((1 - c) * deep, 8), deep)
+    mine = pl.ds(pl.multiple_of(c * deep, 8), deep)
+    push(fin.at[his], row, fsend, frecv, partner)
+    square = part_ref[...]
+    for i in range(2 * deep // 8):
+        for j in range(half // 128):
+            v = fin[pl.ds(8 * i, 8), pl.ds(128 * j, 128)]
+            square = square + v * v
+    tiles[me] = square
+    for j in range(1, world):
+        push(tiles.at[me], tiles.at[me], nsend.at[j], nrecv.at[j], everyone[j - 1])
+    out_ref[:, mycols] = fin[mine, :]
+    got(row, frecv)
+    out_ref[:, hiscols] = row[...]
+    for j in range(1, world):
+        src = lax.rem(me + world - j, world)
+        got(tiles.at[src], nrecv.at[j])
+    total = tiles[0]
+    for j in range(1, world):
+        total = total + tiles[j]
+    total_ref[...] = total
+    for cp in pending:
+        cp.wait_send()
+
+
+def reduce_blocks(grads, part, dp, experts, cid):
+    n = dp * experts
+    chips, rows, cols = grads.shape
+    half = cols // 2
+    bf = jnp.bfloat16
+    return pl.pallas_call(
+        functools.partial(reduce_kernel, dp, experts),
+        out_shape=[jax.ShapeDtypeStruct((rows // 2, cols), jnp.float32), jax.ShapeDtypeStruct((8, 128), jnp.float32)],
+        in_specs=[ANY, VMEM],
+        out_specs=[VMEM, VMEM],
+        scratch_shapes=[
+            pltpu.VMEM((chips, rows, half), bf),
+            pltpu.VMEM((chips, rows, half), bf),
+            pltpu.VMEM((chips // 2, rows, half), bf),
+            pltpu.VMEM((chips // 4, rows, half), bf),
+            pltpu.VMEM((chips // 4 - 1, rows, half), bf),
+            pltpu.VMEM((rows, half), jnp.float32),
+            pltpu.VMEM((rows // 2, half), jnp.float32),
+            pltpu.VMEM((n, 8, 128), jnp.float32),
+            pltpu.SemaphoreType.DMA((chips,)),
+            pltpu.SemaphoreType.DMA((chips,)),
+            pltpu.SemaphoreType.DMA((chips,)),
+            pltpu.SemaphoreType.DMA((chips,)),
+            pltpu.SemaphoreType.DMA((chips,)),
+            pltpu.SemaphoreType.DMA,
+            pltpu.SemaphoreType.DMA,
+            pltpu.SemaphoreType.DMA((n,)),
+            pltpu.SemaphoreType.DMA((n,)),
+        ],
+        compiler_params=pltpu.CompilerParams(collective_id=cid, has_side_effects=True, vmem_limit_bytes=32 * 1024 * 1024),
+        name="reduce_dense",
+    )(grads, part)
+
+
+def fits(dp, experts):
+    return dp == 2 and experts == 16
+
+
+def slot_rows(capacity):
+    return -(-capacity // 8) * 8
+
+
+def fast_shards(
+    dp,
+    experts,
+    tokens,
+    cotangent,
+    expert_choice,
+    priority,
+    projection,
+    projection_first,
+    projection_second,
+    output_weight,
+    output_first,
+    output_second,
+    router_weight,
+    router_first,
+    router_second,
+    vectors,
+    vectors_first,
+    vectors_second,
+    expert_inner,
+    inner_first,
+    inner_second,
+    hidden_bias,
+    hidden_first,
+    hidden_second,
+    expert_outer,
+    outer_first,
+    outer_second,
+    return_bias,
+    return_first,
+    return_second,
+):
+    model_width = tokens.shape[2]
+    patches = tokens.shape[1]
+    capacity = max(2, patches // experts)
+    stride = slot_rows(capacity)
+    slot_count = experts * stride
+    score_scale = HEAD_DIM ** (-0.5)
+    low = jnp.bfloat16
+    my_dp = lax.axis_index("dp")
+    shard_rows = projection.shape[0]
+    wide = 3 * model_width
+    used = wide + model_width + experts + vectors.shape[0]
+    packed = jnp.concatenate(
+        [projection, output_weight, router_weight, vectors.T, jnp.zeros((shard_rows, -used % 128), jnp.float32)], axis=1
+    ).astype(low)
+    gathered = gather_blocks(packed, dp, experts, 1).reshape(model_width, packed.shape[1])
+    whole_projection = gathered[:, :wide]
+    whole_output = gathered[:, wide : wide + model_width]
+    whole_router = gathered[:, wide + model_width : wide + model_width + experts]
+    vector_rows = gathered[:, wide + model_width + experts : used].T.astype(jnp.float32)
+    inner_low = expert_inner[0].astype(low)
+    hidden_low = hidden_bias[0].astype(low)
+    outer_low = expert_outer[0].astype(low)
+    return_low = return_bias[0].astype(low)
+    image_rows = tokens[0].astype(jnp.float32)
+    normed_one, norm_back_one = jax.vjp(layer_norm, image_rows, vector_rows[0], vector_rows[1])
+    normed_low = normed_one.astype(low)
+    projected = mixed_dot(normed_low, whole_projection)
+    queries = (projected[:, :model_width] + vector_rows[2]).astype(low).reshape(patches, HEADS, HEAD_DIM)
+    key_rows = projected[:, model_width : 2 * model_width].astype(low).reshape(patches, HEADS, HEAD_DIM)
+    value_rows = (projected[:, 2 * model_width :] + vector_rows[3]).astype(low).reshape(patches, HEADS, HEAD_DIM)
+    scores = jnp.einsum("qhd,khd->hqk", queries, key_rows, preferred_element_type=jnp.float32) * score_scale
+    score_top = jnp.max(scores, axis=-1, keepdims=True)
+    raised = jnp.exp(scores - score_top)
+    totals = jnp.sum(raised, axis=-1, keepdims=True)
+    attention = raised / totals
+    log_total = score_top + jnp.log(totals)
+    context = (
+        jnp.einsum("hqk,khd->qhd", attention.astype(low), value_rows, preferred_element_type=jnp.float32)
+        .reshape(patches, model_width)
+        .astype(low)
+    )
+    middle = image_rows + (mixed_dot(context, whole_output) + vector_rows[4])
+    normed_two, norm_back_two = jax.vjp(layer_norm, middle, vector_rows[5], vector_rows[6])
+    second_low = normed_two.astype(low)
+    logits = mixed_dot(second_low, whole_router)
+    chosen = expert_choice[0]
+
+    def gate_choice(values):
+        return select_gates(values, chosen, experts)
+
+    gate_values, gate_back = jax.vjp(gate_choice, logits)
+    packed_slot, kept_mask = assign_slots(chosen, priority[0], experts, capacity)
+    flat_slot = packed_slot + chosen * (stride - capacity)
+    matches = slot_matches(flat_slot, kept_mask, slot_count)
+    slot_table = jnp.any(matches, axis=2).astype(low)
+    dispatched = mixed_dot(slot_table, second_low).astype(low).reshape(experts, stride, model_width)
+    upstream = cotangent[0].astype(jnp.float32)
+    weighted = jnp.where(kept_mask, gate_values, 0.0)
+    slot_gate = jnp.sum(jnp.where(matches, weighted[None, :, :], 0.0), axis=(1, 2))
+    slot_grad = (mixed_dot(slot_table, cotangent[0]) * slot_gate[:, None]).astype(low)
+    arrived, sent_grad = dispatch([dispatched, slot_grad.reshape(experts, stride, model_width)], dp, experts, 2)
+    arrived = arrived.reshape(dp * slot_count, model_width)
+    sent_grad = sent_grad.reshape(dp * slot_count, model_width)
+    pre_act = mixed_dot(arrived, inner_low) + hidden_low.astype(jnp.float32)
+    activated, gelu_back = jax.vjp(smooth_gate, pre_act)
+    active_low = activated.astype(low)
+    part = model_width // dp
+    own_columns = jnp.arange(model_width) // part == my_dp
+    return_wide = jnp.where(own_columns, jnp.tile(return_low.astype(jnp.float32), dp), 0.0)
+    expert_part = (mixed_dot(active_low, outer_low) + return_wide).astype(low)
+    active_grad = columns_product(sent_grad, outer_low)
+    (pre_grad,) = gelu_back(active_grad)
+    pre_low = pre_grad.astype(low)
+    row_part = columns_product(pre_low, inner_low).astype(low)
+    outer_grad = rows_product(active_low, sent_grad)[None]
+    inner_grad = rows_product(arrived, pre_low)[None]
+    hidden_grad = jnp.sum(pre_low, axis=0, dtype=jnp.float32)[None]
+    return_sums = jnp.sum(sent_grad, axis=0, dtype=jnp.float32)
+    return_grad = lax.dynamic_slice_in_dim(return_sums, my_dp * part, part)[None]
+    back = (dp, experts, stride, model_width)
+    returned, back_rows = give_back([expert_part.reshape(back), row_part.reshape(back)], dp, experts, 3)
+    returned = returned.reshape(slot_count, model_width)
+    back_rows = back_rows.reshape(slot_count, model_width)
+    picked = returned[flat_slot].astype(jnp.float32)
+    final = middle + jnp.sum(weighted[:, :, None] * picked, axis=1)
+    block_output = final.astype(low)[None]
+    gate_grad = jnp.where(kept_mask, jnp.sum(upstream[:, None, :] * picked, axis=2), 0.0)
+    (logit_grad,) = gate_back(gate_grad)
+    logit_low = logit_grad.astype(low)
+    router_grad = rows_product(second_low, logit_low)
+    second_grad = rows_product(slot_table, back_rows) + columns_product(logit_low, whole_router)
+    middle_part, gain_two_grad, bias_two_grad = norm_back_two(second_grad)
+    middle_grad = upstream + middle_part
+    branch_low = middle_grad.astype(low)
+    output_grad = rows_product(context, branch_low)
+    out_bias_grad = jnp.sum(branch_low, axis=0, dtype=jnp.float32)
+    context_grad = columns_product(branch_low, whole_output).astype(low).reshape(patches, HEADS, HEAD_DIM)
+    scores = jnp.einsum("qhd,khd->hqk", queries, key_rows, preferred_element_type=jnp.float32) * score_scale
+    attention = jnp.exp(scores - log_total)
+    attention_grad = jnp.einsum("qhd,khd->hqk", context_grad, value_rows, preferred_element_type=jnp.float32)
+    value_grad = jnp.einsum(
+        "hqk,qhd->khd", attention.astype(low), context_grad, preferred_element_type=jnp.float32
+    ).astype(low)
+    centered = jnp.sum(attention * attention_grad, axis=-1, keepdims=True)
+    score_grad = (attention * (attention_grad - centered)).astype(low)
+    query_grad = (
+        (jnp.einsum("hqk,khd->qhd", score_grad, key_rows, preferred_element_type=jnp.float32) * score_scale)
+        .astype(low)
+        .reshape(patches, model_width)
+    )
+    key_grad = (
+        (jnp.einsum("hqk,qhd->khd", score_grad, queries, preferred_element_type=jnp.float32) * score_scale)
+        .astype(low)
+        .reshape(patches, model_width)
+    )
+    value_flat = value_grad.reshape(patches, model_width)
+    joined_grad = jnp.concatenate([query_grad, key_grad, value_flat], axis=1)
+    projection_grad = rows_product(normed_low, joined_grad)
+    normed_grad = columns_product(joined_grad, whole_projection)
+    input_part, gain_one_grad, bias_one_grad = norm_back_one(normed_grad)
+    input_grad = (middle_grad + input_part)[None]
+    vector_grad = jnp.stack(
+        [
+            gain_one_grad,
+            bias_one_grad,
+            jnp.sum(query_grad, axis=0, dtype=jnp.float32),
+            jnp.sum(value_flat, axis=0, dtype=jnp.float32),
+            out_bias_grad,
+            gain_two_grad,
+            bias_two_grad,
+        ]
+    )
+    expert_grads = (inner_grad, hidden_grad, outer_grad, return_grad)
+    expert_square = jnp.sum(inner_grad * inner_grad)
+    for gradient in expert_grads[1:]:
+        expert_square = expert_square + jnp.sum(gradient * gradient)
+    chips = dp * experts // 2
+    local_grads = jnp.concatenate(
+        [
+            projection_grad.astype(low),
+            output_grad.astype(low),
+            router_grad.astype(low),
+            vector_grad.T.astype(low),
+            jnp.zeros((model_width, -used % 256), low),
+        ],
+        axis=1,
+    ).reshape(chips, 2 * shard_rows, -1)
+    square_tile = jnp.where(jnp.arange(1024).reshape(8, 128) == 0, expert_square, 0.0)
+    dense, squares = reduce_blocks(local_grads, square_tile, dp, experts, 4)
+    grad_norm = jnp.sqrt(jnp.sum(squares))
+    clip_factor = THRESHOLD / jnp.maximum(grad_norm, THRESHOLD)
+    projection_new = adam_update(
+        projection, projection_first, projection_second, dense[:, :wide], clip_factor, RATE_PROJECTION, DECAY
+    )
+    output_new = adam_update(
+        output_weight,
+        output_first,
+        output_second,
+        dense[:, wide : wide + model_width],
+        clip_factor,
+        RATE_OUTPUT,
+        DECAY,
+    )
+    router_new = adam_update(
+        router_weight,
+        router_first,
+        router_second,
+        dense[:, wide + model_width : wide + model_width + experts],
+        clip_factor,
+        RATE_ROUTER,
+        DECAY,
+    )
+    vectors_new = adam_update(
+        vectors,
+        vectors_first,
+        vectors_second,
+        dense[:, wide + model_width + experts : used].T,
+        clip_factor,
+        RATE_VECTORS,
+        0.0,
+    )
+    inner_new = adam_update(expert_inner, inner_first, inner_second, inner_grad, clip_factor, RATE_INNER, DECAY)
+    hidden_new = adam_update(hidden_bias, hidden_first, hidden_second, hidden_grad, clip_factor, RATE_HIDDEN, 0.0)
+    outer_new = adam_update(expert_outer, outer_first, outer_second, outer_grad, clip_factor, RATE_OUTER, DECAY)
+    return_new = adam_update(return_bias, return_first, return_second, return_grad, clip_factor, RATE_RETURN, 0.0)
+    return (
+        block_output,
+        input_grad,
+        grad_norm,
+        *projection_new,
+        *output_new,
+        *router_new,
+        *vectors_new,
+        *inner_new,
+        *hidden_new,
+        *outer_new,
+        *return_new,
+    )
+
+
 def solution(mesh):
+    dp, experts = mesh.shape["dp"], mesh.shape["expert"]
+    body = functools.partial(fast_shards, dp, experts) if fits(dp, experts) else shards
     return jax.shard_map(
-        shards,
+        body,
         mesh=mesh,
         in_specs=(
             P(("dp", "expert"), None, None),

time: 869 us -> 477 us (0.55)
  waiting for transfers between devices: 355 us -> 0 us
  Pallas kernels: 0 us -> 203 us
  blocking collectives: 178 us -> 0 us
  starting transfers between devices: 23.8 us -> 0 us
  between operations: 22.9 us -> 6.45 us
  other arithmetic: 103 us -> 87.2 us
  matrix products: 132 us -> 122 us
    pallas_call x0 -> x4, Pallas kernels: none -> 203 us  [the longest x1 61.7 us: give_back(): pl.pallas_call(functools.partial(return_kernel, dp, experts), out_shape=[...]
    reduce_scatter x6 -> x0, waiting for transfers between devices: 189 us -> none  [the longest x1 60.4 us: shards(): lax.psum_scatter(partial_grads[0].astype(jnp.bfloat16), 'expert', scatter...]
    all_gather x7 -> x0, blocking collectives: 76.3 us -> none  [the longest x1 22.1 us: shards(): lax.all_gather(dense_shards[1], 'expert', axis=0, tiled=True)]
    unnamed x1 -> x0, blocking collectives: 61.2 us -> none
    unnamed x19 -> x0, waiting for transfers between devices: 56.8 us -> none
    all_gather x5 -> x0, waiting for transfers between devices: 54.6 us -> none  [the longest x1 44.9 us: shards(): lax.all_gather(dense_shards[0], 'expert', axis=0, tiled=True)]
    all_to_all x4 -> x0, waiting for transfers between devices: 54 us -> none  [the longest x1 16.4 us: shards(): lax.all_to_all(slot_grad.reshape(experts, capacity, model_width), 'expert...]
    psum x1 -> x0, blocking collectives: 40 us -> none  [shards(): square_total = lax.psum(local_square, ('dp', 'expert'))]
  transfers between devices with their start and end apart: 19 -> 0, of which waited for: 14 -> 0; matrix products, arithmetic and copies ran while one was open for 22% -> 0% of each run, Pallas kernels for 0% -> 0%
where the time goes in v1:
time: 477 us; the launch traced here: 473 us
  Pallas kernels  203 us (43%)
  matrix products  122 us (26%)
  other arithmetic  87.2 us (18%)
  local copies, waits for them, and re-layouts  54.2 us (11%)
  between operations  6.45 us (1%)
    pallas_call x1, Pallas kernels, give_back(): pl.pallas_call(functools.partial(return_kernel, dp, experts), out_shape=[...  61.7 us
    pallas_call x1, Pallas kernels, dispatch(): pl.pallas_call(functools.partial(dispatch_kernel, dp, experts), out_shape...  58.5 us
    pallas_call x1, Pallas kernels, reduce_blocks(): pl.pallas_call(functools.partial(reduce_kernel, dp, experts), out_shape=[...  49.3 us
    pallas_call x1, Pallas kernels, gather_blocks(): pl.pallas_call(functools.partial(gather_kernel, dp, experts), out_shape=j...  33.7 us
    sub x8, other arithmetic, adam_update(): weight - step_rate * (first_hat / (jnp.sqrt(second_hat) + ADAM_EPS) + dec...  26.4 us
    dot_general x7, matrix products, mixed_dot(): return jnp.dot(left, right, preferred_element_type=jnp.float32)  26 us
    dot_general x6, matrix products, rows_product(): lax.dot_general(left, right, (((0,), (0,)), ((), ())), preferred_element_...  25.6 us
    dot_general x5, matrix products, columns_product(): lax.dot_general(left, right, (((1,), (1,)), ((), ())), preferred_element_...  24.9 us

profile of v1, /device:TPU:0, one launch (start us, length us, event | category | flops | bytes accessed | tf_op | source)
XLA Modules:
  0.0 472.9 jit_solution(8448174649237919462)
XLA Ops:
  5.3 1.6 fusion.49
  24.0 33.7 %gather_dense.1 = bf16[32,24,3200]{2,1,0:T(8,128)(2,1)} custom-call(bf16[24,3200]{1,0:T(8,128)(2,1)} %concatenate.10.in_ref), custom_call_target="tpu_custom_call" | custom-call | tf_op jit(solution)/shard_map/gather_dense/pallas_call | solution.py:563
  59.0 4.4 fusion.22
  66.3 1.9 copy.199
  68.2 2.6 copy.197
  70.8 7.4 %multiply_reduce_fusion.1 = (f32[12,576]{1,0:T(8,128)S(1)}, f32[12,576,576]{1,2,0:T(8,128)}) fusion(bf16[576,12,64]{0,2,1:T(8,128)(2,1)S(1)} %bitcast.171, bf16[576,12,64]{0,2,1:T(8,128)(2,1)S(1)} %bitcast.167), kind=kOutput, calls=%fused_computation.7 | convolution fusion | flops 517563648 | bytes 17722368 | tf_op jit(solution)/shard_map/qhd,khd->hqk/dot_general | solution.py:888
  78.2 9.2 %fusion = f32[12,576]{1,0:T(8,128)S(1)} fusion(f32[12,576,576]{1,2,0:T(8,128)} %get-tuple-element.226, f32[12,576]{1,0:T(8,128)S(1)} %get-tuple-element.225), kind=kLoop, calls=%fused_computation.6 | loop fusion | flops 11937024 | bytes 15980544 | tf_op jit(solution)/shard_map/reduce_sum | solution.py:891
  88.0 8.6 %fusion.53 = bf16[12,64,576]{2,1,0:T(8,128)(2,1)S(1)} fusion(bf16[576,12,64]{0,2,1:T(8,128)(2,1)S(1)} %bitcast.187, f32[12,576,576]{1,2,0:T(8,128)} %get-tuple-element.226, f32[12,576]{1,0:T(8,128)S(1)} %fusion, f32[12,576]{1,0:T(8,128)S(1)} %get-tuple-element.225), kind=kOutput, calls=%fused_computation.96 | convolution fusion | flops 525975552 | bytes 17750016 | tf_op jit(solution)/shard_map/hqk,khd->qhd/dot_general | solution.py:895
  96.6 2.7 fusion.111
  100.9 1.5 fusion.112
  104.9 2.0 multiply_convert_fusion.4
  106.9 2.0 convolution_convert_fusion.3
  108.9 58.5 %dispatch_rows.1 = (bf16[2,16,40,768]{3,2,1,0:T(8,128)(2,1)}, bf16[2,16,40,768]{3,2,1,0:T(8,128)(2,1)}) custom-call(bf16[16,40,768]{2,1,0:T(8,128)(2,1)} %bitcast.195, bf16[16,40,768]{2,1,0:T(8,128)(2,1)} %bitcast.194), custom_call_target="tpu_custom_call" | custom-call | tf_op jit(solution)/shard_map/dispatch_rows/pallas_call | solution.py:626
  167.5 1.9 convert_reduce_fusion.1
  170.1 5.9 %convolution_add_fusion = f32[1280,1536]{1,0:T(8,128)S(1)} fusion(bf16[1280,768]{1,0:T(8,128)(2,1)} %bitcast.205, f32[1536]{0:T(1024)S(1)} %convert_reduce_fusion.3, f32[1,768,1536]{2,1,0:T(8,128)} %param.44), kind=kOutput, calls=%fused_computation.11 | convolution fusion | flops 3023044608 | bytes 14555136 | tf_op jit(solution)/shard_map/dot_general | solution.py:42
  176.0 7.4 %add_convert_fusion = bf16[1280,768]{1,0:T(8,128)(2,1)S(1)} fusion(f32[768]{0:T(1024)S(1)} %fusion.85, f32[1,1536,768]{2,1,0:T(8,128)} %param.50, f32[1280,1536]{1,0:T(8,128)S(1)} %convolution_add_fusion), kind=kOutput, calls=%fused_computation.41 | convolution fusion | flops 3040739328 | bytes 14552064 | tf_op jit(solution)/shard_map/dot_general | solution.py:42
  183.4 9.2 %convert_reduce_fusion = (f32[1536]{0:T(1024)S(1)}, bf16[1280,1536]{1,0:T(8,128)(2,1)S(1)}) fusion(f32[1280,1536]{1,0:T(8,128)S(1)} %convolution_add_fusion, bf16[1280,768]{1,0:T(8,128)(2,1)S(1)} %bitcast.190, f32[1,1536,768]{2,1,0:T(8,128)S(1)} %bitcast.181), kind=kOutput, calls=%fused_computation.23 | convolution fusion | flops 3064330752 | bytes 18487296 | tf_op jit(solution)/shard_map/dot_general | solution.py:52
  192.7 6.6 %multiply_reduce_fusion.2 = (f32[]{:T(128)}, f32[1536,768]{1,0:T(8,128)}) fusion(bf16[1280,768]{1,0:T(8,128)(2,1)S(1)} %bitcast.191, f32[1280,1536]{1,0:T(8,128)S(1)} %convolution_add_fusion), kind=kOutput, calls=%fused_computation.38 | convolution fusion | flops 3039952896 | bytes 14548996 | tf_op jit(solution)/shard_map/dot_general | solution.py:46
  199.9 4.4 convolution_convert_fusion.1
  204.3 5.7 %multiply_reduce_fusion.3 = (f32[]{:T(128)}, f32[768,1536]{1,0:T(8,128)}) fusion(bf16[1280,768]{1,0:T(8,128)(2,1)S(1)} %bitcast.206, bf16[1280,1536]{1,0:T(8,128)(2,1)S(1)} %get-tuple-element.242), kind=kOutput, calls=%fused_computation.39 | convolution fusion | flops 3022258176 | bytes 10616836 | tf_op jit(solution)/shard_map/dot_general | solution.py:46
  212.7 1.5 copy-done.1
  214.2 61.7 %return_rows.1 = (bf16[16,40,768]{2,1,0:T(8,128)(2,1)S(1)}, bf16[16,40,768]{2,1,0:T(8,128)(2,1)S(1)}) custom-call(bf16[2,16,40,768]{3,2,1,0:T(8,128)(2,1)S(1)} %bitcast.164, bf16[2,16,40,768]{3,2,1,0:T(8,128)(2,1)S(1)} %bitcast.165), custom_call_target="tpu_custom_call" | custom-call | tf_op jit(solution)/shard_map/return_rows/pallas_call | solution.py:686
  275.9 2.1 fusion.113
  278.0 4.5 gather_fusion
  282.6 3.2 reshape.370
  285.8 9.5 %multiply_reduce_fusion.4 = (f32[576,2]{1,0:T(8,128)S(1)}, f32[576,768]{1,0:T(8,128)}) fusion(f32[576,2,768]{2,1,0:T(2,128)} %reshape.370, f32[576,768]{1,0:T(8,128)} %bitcast_convert_fusion, f32[576,2]{1,0:T(8,128)} %copy.201), kind=kLoop, calls=%fused_computation.42 | loop fusion | flops 3095424 | bytes 7087104 | tf_op jit(solution)/shard_map/reduce_sum | solution.py:944
  296.5 2.5 multiply_reduce_fusion.6
  299.1 2.4 fusion.109
  302.7 1.6 copy.210
  304.2 1.5 fusion.107
  306.4 3.3 convolution_convert_fusion.2
  309.7 3.1 convolution_convert_fusion.4
  312.7 1.5 copy.204
  314.3 10.2 %bitcast_reduce_fusion = (bf16[12,64]{1,0:T(8,128)(2,1)S(1)}, bf16[12,64,576]{2,1,0:T(8,128)(2,1)}) fusion(bf16[576,12,64]{0,2,1:T(8,128)(2,1)S(1)} %bitcast.169, f32[12,576,576]{1,2,0:T(8,128)} %get-tuple-element.226, f32[12,576]{1,0:T(8,128)S(1)} %copy-done.24), kind=kOutput, calls=%fused_computation.108 | convolution fusion | flops 522435840 | bytes 17723904 | tf_op jit(solution)/shard_map/hqk,qhd->khd/dot_general | solution.py:958
  325.1 11.8 %multiply_reduce_fusion = (f32[12,576]{1,0:T(8,128)S(1)}, f32[12,576,576]{1,2,0:T(8,128)}) fusion(f32[12,576,576]{1,2,0:T(8,128)} %get-tuple-element.226, f32[12,576]{1,0:T(8,128)S(1)} %copy-done.24, bf16[576,12,64]{0,2,1:T(8,128)(2,1)S(1)} %bitcast.170, bf16[576,12,64]{0,2,1:T(8,128)(2,1)} %bitcast.186), kind=kOutput, calls=%fused_computation.2 | convolution fusion | flops 525526272 | bytes 33675264 | tf_op jit(solution)/shard_map/qhd,khd->hqk/dot_general | solution.py:957
  337.0 12.8 %multiply_convert_fusion = bf16[12,576,576]{1,2,0:T(8,128)(2,1)S(1)} fusion(f32[12,576,576]{1,2,0:T(8,128)} %get-tuple-element.233, f32[12,576,576]{1,2,0:T(8,128)} %get-tuple-element.226, f32[12,576]{1,0:T(8,128)S(1)} %get-tuple-element.232, f32[12,576]{1,0:T(8,128)S(1)} %copy-done.24), kind=kLoop, calls=%fused_computation.1 | loop fusion | flops 19906560 | bytes 39868416 | tf_op jit(solution)/shard_map/convert_element_type | solution.py:962
  349.9 3.6 multiply_convert_fusion.2
  353.5 2.6 bitcast_reduce_fusion.1
  356.9 5.7 %fusion.98 = (bf16[768]{0:T(1024)(128)(2,1)S(1)}, f32[576]{0:T(1024)S(1)}, f32[576,768]{1,0:T(8,128)S(1)}) fusion(f32[768]{0:T(1024)S(1)} %copy-done.51, f32[576]{0:T(1024)S(1)} %copy-done.39, bf16[1,576,768]{2,1,0:T(8,128)(2,1)S(1)} %copy-done.5, bf16[768,3200]{1,0:T(8,128)(2,1)} %bitcast.179, bf16[576,768]{0,1:T(8,128)(2,1)} %bitcast.192, ...), kind=kOutput, calls=%fused_computation.209 | convolution fusion | flops 2049047296 | bytes 9151488 | tf_op jit(solution)/shard_map/dot_general | solution.py:52
  363.8 1.5 fusion.48
  365.9 1.4 stack.27
  368.0 3.5 add_bitcast_fusion
  372.3 7.0 %convolution_convert_fusion = bf16[768,2304]{1,0:T(8,128)(2,1)} fusion(bf16[576,768]{0,1:T(8,128)(2,1)} %bitcast.193, bf16[576,768]{0,1:T(8,128)(2,1)} %bitcast.197, bf16[576,768]{0,1:T(8,128)(2,1)} %bitcast.189, bf16[1,576,768]{2,1,0:T(8,128)(2,1)S(1)} %copy-done.5, f32[768]{0:T(1024)} %copy-done.68, f32[768]{0:T(1024)S(1)} %copy-done.51, ...), kind=kOutput, calls=%fused_computation.29 | convolution fusion | flops 2050818048 | bytes 7088640 | tf_op jit(solution)/shard_map/dot_general | solution.py:46
  379.4 8.2 %concatenate.12 = bf16[768,3328]{1,0:T(8,128)(2,1)} concatenate(bf16[768,2304]{1,0:T(8,128)(2,1)} %convolution_convert_fusion, bf16[768,768]{1,0:T(8,128)(2,1)S(1)} %copy-done.19, bf16[768,16]{1,0:T(8,128)(2,1)S(1)} %copy-done.23, bf16[768,7]{1,0:T(8,128)(2,1)S(1)} %bitcast.198, bf16[768,233]{1,0:T(8,128)(2,1)S(1)} %broadcast_in_dim.124), dimensions={1} | concatenate | bytes 10223616 | tf_op jit(solution)/shard_map/concatenate | solution.py:995
  387.7 2.5 copy-done
  390.3 49.3 %reduce_dense.1 = (f32[24,3328]{1,0:T(8,128)S(1)}, f32[8,128]{1,0:T(8,128)S(1)}) custom-call(bf16[16,48,3328]{2,1,0:T(8,128)(2,1)S(1)} %bitcast.163, f32[8,128]{1,0:T(8,128)S(1)} %fusion.86.part_ref), custom_call_target="tpu_custom_call" | custom-call | tf_op jit(solution)/shard_map/reduce_dense/pallas_call | solution.py:789
  448.2 13.1 %multiply_subtract_fusion = (f32[1,1536,768]{2,1,0:T(8,128)}, f32[1,1536,768]{2,1,0:T(8,128)}, f32[1,1536,768]{2,1,0:T(8,128)}) fusion(f32[1,1536,768]{2,1,0:T(8,128)} %param.50, f32[1536,768]{1,0:T(8,128)} %get-tuple-element.244, f32[]{:T(128)S(6)} %div.216, f32[1,1536,768]{2,1,0:T(8,128)} %param.51, f32[1,1536,768]{2,1,0:T(8,128)} %param.52), kind=kLoop, calls=%fused_computation.36 | loop fusion | flops 18874368 | bytes 33030148 | tf_op jit(solution)/shard_map/sub | solution.py:94
  461.3 10.3 %multiply_subtract_fusion.1 = (f32[1,768,1536]{2,1,0:T(8,128)}, f32[1,768,1536]{2,1,0:T(8,128)}, f32[1,768,1536]{2,1,0:T(8,128)}) fusion(f32[1,768,1536]{2,1,0:T(8,128)S(1)} %bitcast.185, f32[768,1536]{1,0:T(8,128)} %get-tuple-element.240, f32[]{:T(128)S(6)} %div.216, f32[1,768,1536]{2,1,0:T(8,128)} %param.45, f32[1,768,1536]{2,1,0:T(8,128)} %param.46), kind=kLoop, calls=%fused_computation.37 | loop fusion | flops 18874368 | bytes 33030148 | tf_op jit(solution)/shard_map/sub | solution.py:94
  (254 shorter events, 47.0 us)
Async XLA Ops:
  0.7 22.0 %copy-start.12 = (bf16[1,576,768]{2,1,0:T(8,128)(2,1)S(1)}, bf16[1,576,768]{2,1,0:T(8,128)(2,1)}, u32[]{:S(2)}) copy-start(bf16[1,576,768]{2,1,0:T(8,128)(2,1)} %param.29) | copy-start | bytes 2654212
  5.3 53.7 %copy-start.38 = (f32[576]{0:T(1024)}, f32[576]{0:T(1024)S(1)}, u32[]{:S(2)}) copy-start(f32[576]{0:T(1024)S(1)} %broadcast_multiply_fusion.2) | copy-start | bytes 6916
  6.9 13.5 %copy-start.54 = (f32[576]{0:T(1024)}, f32[576]{0:T(1024)S(1)}, u32[]{:S(2)}) copy-start(f32[576]{0:T(1024)S(1)} %fusion.49) | copy-start | bytes 6916
  6.9 52.1 %copy-start.52 = (f32[576]{0:T(1024)}, f32[576]{0:T(1024)S(1)}, u32[]{:S(2)}) copy-start(f32[576]{0:T(1024)S(1)} %fusion.88) | copy-start | bytes 6916
  8.9 94.3 %copy-start.42 = (pred[2,576]{1,0:T(4,128)(4,1)}, pred[2,576]{1,0:T(4,128)(4,1)S(1)}, u32[]{:S(2)}) copy-start(pred[2,576]{1,0:T(4,128)(4,1)S(1)} %lt.35) | copy-start | bytes 3460
  21.1 37.9 %copy-start.4 = (bf16[1,576,768]{2,1,0:T(8,128)(2,1)S(1)}, bf16[1,576,768]{2,1,0:T(8,128)(2,1)}, u32[]{:S(2)}) copy-start(bf16[1,576,768]{2,1,0:T(8,128)(2,1)} %param.28) | copy-start | bytes 2654212
  59.0 40.8 %copy-start.34 = (f32[768]{0:T(1024)}, f32[768]{0:T(1024)S(1)}, u32[]{:S(2)}) copy-start(f32[768]{0:T(1024)S(1)} %get-tuple-element.183) | copy-start | bytes 9220
  66.3 11.9 %copy-start.8 = (bf16[576,768]{0,1:T(8,128)(2,1)}, bf16[576,768]{0,1:T(8,128)(2,1)S(1)}, u32[]{:S(2)}) copy-start(bf16[576,768]{0,1:T(8,128)(2,1)S(1)} %copy.198) | copy-start | bytes 2654212
  68.2 10.0 %copy-start.6 = (bf16[576,768]{0,1:T(8,128)(2,1)}, bf16[576,768]{0,1:T(8,128)(2,1)S(1)}, u32[]{:S(2)}) copy-start(bf16[576,768]{0,1:T(8,128)(2,1)S(1)} %copy.199) | copy-start | bytes 2654212
  78.2 9.8 %copy-start.17 = (bf16[576,768]{0,1:T(8,128)(2,1)S(1)}, bf16[576,768]{0,1:T(8,128)(2,1)}, u32[]{:S(2)}) copy-start(bf16[576,768]{0,1:T(8,128)(2,1)} %copy.197) | copy-start | bytes 2654212
  102.5 65.0 %copy-start.28 = (f32[576]{0:T(1024)}, f32[576]{0:T(1024)S(1)}, u32[]{:S(2)}) copy-start(f32[576]{0:T(1024)S(1)} %get-tuple-element.229) | copy-start | bytes 6916
  102.5 65.0 %copy-start.40 = (f32[576]{0:T(1024)}, f32[576]{0:T(1024)S(1)}, u32[]{:S(2)}) copy-start(f32[576]{0:T(1024)S(1)} %fusion.76) | copy-start | bytes 6916
  170.0 13.3 %slice-start = ((s8[4718592]{0:T(1024)(128)(4,1)}), s8[4194304]{0:T(1024)(128)(4,1)S(1)}, s32[]{:S(2)}) async-start(s8[4718592]{0:T(1024)(128)(4,1)} %bitcast.180), calls=%async_computation | async-start | bytes 8388608
  176.0 23.9 %slice-start.2 = ((s8[4718592]{0:T(1024)(128)(4,1)}), s8[4194304]{0:T(1024)(128)(4,1)S(1)}, s32[]{:S(2)}) async-start(s8[4718592]{0:T(1024)(128)(4,1)} %bitcast.182), calls=%async_computation.2 | async-start | bytes 8388608
  183.4 16.5 %slice-start.3 = ((s8[4718592]{0:T(1024)(128)(4,1)}), s8[524288]{0:T(1024)(128)(4,1)S(1)}, s32[]{:S(2)}) async-start(s8[4718592]{0:T(1024)(128)(4,1)} %bitcast.182), calls=%async_computation.3 | async-start | bytes 1048576
  285.7 9.8 %copy-start.21 = (f32[576,16]{0,1:T(8,128)S(1)}, f32[576,16]{0,1:T(8,128)}, u32[]{:S(2)}) copy-start(f32[576,16]{0,1:T(8,128)} %copy-done.20) | copy-start | bytes 110596
  285.8 9.8 %copy-start.29 = (f32[576]{0:T(1024)S(1)}, f32[576]{0:T(1024)}, u32[]{:S(2)}) copy-start(f32[576]{0:T(1024)} %copy-done.28) | copy-start | bytes 6916
  285.8 9.8 %copy-start.64 = (f32[576]{0:T(1024)S(1)}, f32[576]{0:T(1024)}, u32[]{:S(2)}) copy-start(f32[576]{0:T(1024)} %multiply_divide_fusion) | copy-start | bytes 6916
  285.8 9.9 %copy-start.41 = (f32[576]{0:T(1024)S(1)}, f32[576]{0:T(1024)}, u32[]{:S(2)}) copy-start(f32[576]{0:T(1024)} %copy-done.40) | copy-start | bytes 6916
  285.8 9.9 %copy-start.11 = (bf16[576,768]{1,0:T(8,128)(2,1)S(1)}, bf16[576,768]{1,0:T(8,128)(2,1)}, u32[]{:S(2)}) copy-start(bf16[576,768]{1,0:T(8,128)(2,1)} %copy-done.10) | copy-start | bytes 2654212
  285.8 10.7 %copy-start.3 = (f32[576,768]{1,0:T(8,128)S(1)}, f32[576,768]{1,0:T(8,128)}, u32[]{:S(2)}) copy-start(f32[576,768]{1,0:T(8,128)} %copy-done.2) | copy-start | bytes 5308420
  285.8 10.7 %copy-start.35 = (f32[768]{0:T(1024)S(1)}, f32[768]{0:T(1024)}, u32[]{:S(2)}) copy-start(f32[768]{0:T(1024)} %copy-done.34) | copy-start | bytes 9220
  285.8 10.7 %copy-start.37 = (f32[576]{0:T(1024)S(1)}, f32[576]{0:T(1024)}, u32[]{:S(2)}) copy-start(f32[576]{0:T(1024)} %copy-done.36) | copy-start | bytes 6916
  301.5 11.2 %copy-start.58 = (f32[576]{0:T(1024)}, f32[576]{0:T(1024)S(1)}, u32[]{:S(2)}) copy-start(f32[576]{0:T(1024)S(1)} %negate_multiply_fusion.1) | copy-start | bytes 6916
  337.0 12.9 %copy-start.9 = (bf16[576,768]{0,1:T(8,128)(2,1)S(1)}, bf16[576,768]{0,1:T(8,128)(2,1)}, u32[]{:S(2)}) copy-start(bf16[576,768]{0,1:T(8,128)(2,1)} %copy-done.8) | copy-start | bytes 2654212
  356.8 11.1 %copy-start.14 = (bf16[1,576,768]{2,1,0:T(8,128)(2,1)S(1)}, bf16[1,576,768]{2,1,0:T(8,128)(2,1)}, u32[]{:S(2)}) copy-start(bf16[1,576,768]{2,1,0:T(8,128)(2,1)} %param.29) | copy-start | bytes 2654212
  387.7 54.9 %copy-start.65 = (f32[1,384]{1,0:T(1,128)S(1)}, f32[1,384]{1,0:T(1,128)}, u32[]{:S(2)}) copy-start(f32[1,384]{1,0:T(1,128)} %param.53) | copy-start | bytes 4612
  390.1 50.9 %copy-start.63 = (f32[768]{0:T(1024)S(1)}, f32[768]{0:T(1024)}, u32[]{:S(2)}) copy-start(f32[768]{0:T(1024)} %copy-done.62) | copy-start | bytes 9220
  390.1 51.0 %copy-start.60 = (f32[1536]{0:T(1024)S(1)}, f32[1536]{0:T(1024)}, u32[]{:S(2)}) copy-start(f32[1536]{0:T(1024)} %copy-done.59) | copy-start | bytes 18436
  390.1 51.0 %copy-start.47 = (f32[7,24]{0,1:T(8,128)S(1)}, f32[7,24]{0,1:T(8,128)}, u32[]{:S(2)}) copy-start(f32[7,24]{0,1:T(8,128)} %copy.216) | copy-start | bytes 2020
  390.2 51.0 %copy-start.48 = (f32[7,24]{0,1:T(8,128)S(1)}, f32[7,24]{0,1:T(8,128)}, u32[]{:S(2)}) copy-start(f32[7,24]{0,1:T(8,128)} %copy.218) | copy-start | bytes 2020
  390.2 51.0 %copy-start.49 = (f32[7,24]{0,1:T(8,128)S(1)}, f32[7,24]{0,1:T(8,128)}, u32[]{:S(2)}) copy-start(f32[7,24]{0,1:T(8,128)} %copy.220) | copy-start | bytes 2020
  390.2 51.7 %copy-start.44 = (f32[24,16]{1,0:T(8,128)S(1)}, f32[24,16]{1,0:T(8,128)}, u32[]{:S(2)}) copy-start(f32[24,16]{1,0:T(8,128)} %copy.211) | copy-start | bytes 4612
  390.2 51.7 %copy-start.45 = (f32[24,16]{1,0:T(8,128)S(1)}, f32[24,16]{1,0:T(8,128)}, u32[]{:S(2)}) copy-start(f32[24,16]{1,0:T(8,128)} %copy.213) | copy-start | bytes 4612
  390.2 51.7 %copy-start.46 = (f32[24,16]{1,0:T(8,128)S(1)}, f32[24,16]{1,0:T(8,128)}, u32[]{:S(2)}) copy-start(f32[24,16]{1,0:T(8,128)} %copy.215) | copy-start | bytes 4612
  390.2 52.4 %copy-start.69 = (f32[1,384]{1,0:T(1,128)S(1)}, f32[1,384]{1,0:T(1,128)}, u32[]{:S(2)}) copy-start(f32[1,384]{1,0:T(1,128)} %param.54) | copy-start | bytes 4612
  390.2 52.4 %copy-start.70 = (f32[1,384]{1,0:T(1,128)S(1)}, f32[1,384]{1,0:T(1,128)}, u32[]{:S(2)}) copy-start(f32[1,384]{1,0:T(1,128)} %param.55) | copy-start | bytes 4612
  390.2 55.6 %copy-start.61 = (f32[1,1536]{1,0:T(1,128)S(1)}, f32[1,1536]{1,0:T(1,128)}, u32[]{:S(2)}) copy-start(f32[1,1536]{1,0:T(1,128)} %param.47) | copy-start | bytes 18436
  390.2 55.6 %copy-start.66 = (f32[1,1536]{1,0:T(1,128)S(1)}, f32[1,1536]{1,0:T(1,128)}, u32[]{:S(2)}) copy-start(f32[1,1536]{1,0:T(1,128)} %param.48) | copy-start | bytes 18436
  390.3 55.6 %copy-start.67 = (f32[1,1536]{1,0:T(1,128)S(1)}, f32[1,1536]{1,0:T(1,128)}, u32[]{:S(2)}) copy-start(f32[1,1536]{1,0:T(1,128)} %param.49) | copy-start | bytes 18436
  390.3 56.3 %copy-start.25 = (f32[24,768]{1,0:T(8,128)S(1)}, f32[24,768]{1,0:T(8,128)}, u32[]{:S(2)}) copy-start(f32[24,768]{1,0:T(8,128)} %param.35) | copy-start | bytes 221188
  390.3 56.3 %copy-start.32 = (f32[24,768]{1,0:T(8,128)S(1)}, f32[24,768]{1,0:T(8,128)}, u32[]{:S(2)}) copy-start(f32[24,768]{1,0:T(8,128)} %param.36) | copy-start | bytes 221188
  390.3 56.2 %copy-start.33 = (f32[24,768]{1,0:T(8,128)S(1)}, f32[24,768]{1,0:T(8,128)}, u32[]{:S(2)}) copy-start(f32[24,768]{1,0:T(8,128)} %param.37) | copy-start | bytes 221188
  390.3 57.0 %copy-start.22 = (f32[24,2304]{1,0:T(8,128)S(1)}, f32[24,2304]{1,0:T(8,128)}, u32[]{:S(2)}) copy-start(f32[24,2304]{1,0:T(8,128)} %param.32) | copy-start | bytes 663556
  390.3 56.9 %copy-start.26 = (f32[24,2304]{1,0:T(8,128)S(1)}, f32[24,2304]{1,0:T(8,128)}, u32[]{:S(2)}) copy-start(f32[24,2304]{1,0:T(8,128)} %param.33) | copy-start | bytes 663556
  390.3 56.9 %copy-start.27 = (f32[24,2304]{1,0:T(8,128)S(1)}, f32[24,2304]{1,0:T(8,128)}, u32[]{:S(2)}) copy-start(f32[24,2304]{1,0:T(8,128)} %param.34) | copy-start | bytes 663556
  390.3 71.0 %slice-start.4 = ((s8[4718592]{0:T(1024)(128)(4,1)}), s8[524288]{0:T(1024)(128)(4,1)S(1)}, s32[]{:S(2)}) async-start(s8[4718592]{0:T(1024)(128)(4,1)} %bitcast.184), calls=%async_computation.4 | async-start | bytes 1048576
  448.2 13.1 %slice-start.5 = ((s8[4718592]{0:T(1024)(128)(4,1)}), s8[4194304]{0:T(1024)(128)(4,1)S(1)}, s32[]{:S(2)}) async-start(s8[4718592]{0:T(1024)(128)(4,1)} %bitcast.184), calls=%async_computation.5 | async-start | bytes 8388608
  (31 other events, 162.1 us)
